TPU v7x, 256 devices: a whole 4x4x8 slice. The times are simulated.
256 devices in a mesh: fsdp: 64 (over z, y, core), rep: 4 (over x).
Axes of the slice: x: 4, y: 4, z: 8, core: 2. Of those that a mesh axis runs over, the one named last changes fastest.
Arguments:
- grad: float32 [4096, 12288], P('fsdp'), may hold values from -6 to 6
- left_stat: float32 [192, 512, 512], P('fsdp', 'rep'), may hold values from -0.5 to 2, as said below
- right_stat: float32 [192, 512, 512], P('fsdp', 'rep'), may hold values from -0.5 to 2, as said below
- left_root: float32 [192, 512, 512], P('fsdp', 'rep'), may hold values from -0.5 to 1.6, as said below
- right_root: float32 [192, 512, 512], P('fsdp', 'rep'), may hold values from -0.5 to 1.6, as said below
Outputs:
- preconditioned: float32 [4096, 12288], P('fsdp')
- left_next: float32 [192, 512, 512], P('fsdp', 'rep')
- right_next: float32 [192, 512, 512], P('fsdp', 'rep')
Inputs may be any that keep to these rules, and one draw needn't show every extreme that they name: `left_stat`: every block is symmetric. `right_stat`: every block is symmetric. `left_root`: every block is symmetric. `right_root`: every block is symmetric.
All inputs are finite; a program needn't handle non-finite values.
Results may differ from a plain program's by a relative error of at most 0.00007.
Values sent between devices are 32-bit elements; how exact they have to be, the bound alone decides.
No kernel may reach another device: no remote copies, remote signals or barrier semaphores. Data moves between devices by JAX's collectives and lax.ppermute only.
A program may use at most 64 MiB of HBM per device.

v0:
```python
import jax
import jax.numpy as jnp
from jax import lax
from jax.experimental import pallas as pl
from jax.experimental.pallas import tpu as pltpu
from jax.sharding import PartitionSpec as P

STAT_DECAY = 0.9
F32 = jnp.float32
BF16 = jnp.bfloat16
BAND = 128
BLOCK = 512
SLOTS = 3
OWNED = SLOTS * BLOCK
REPLICAS = 4
BANDED = (0, 1)
FILLED = 2
SHIFTS = (1, 3, 2)
HBM = pl.BlockSpec(memory_space=pltpu.HBM)
PARAMS = pltpu.CompilerParams(vmem_limit_bytes=63 * 1024 * 1024 + 512 * 1024)


def array(*shape, dtype=F32):
    return jax.ShapeDtypeStruct(shape, dtype)


def cost(flops, data):
    return pl.CostEstimate(flops=1, bytes_accessed=1, transcendentals=0)


def at(index, size=BAND):
    return pl.ds(pl.multiple_of(index * size, size), size)


def split(x):
    high = x.astype(BF16)
    return high, (x - high.astype(F32)).astype(BF16)


def stacked(x):
    return jnp.concatenate(split(x), axis=0)


def dot_stacked(a, b, dims):
    rows = a.shape[0] // 2

    def one(x, y):
        return lax.dot_general(x, y, (dims, ((), ())), preferred_element_type=F32)

    both = one(a, b[0])
    return both[:rows] + (both[rows:] + one(a[:rows], b[1]))


def dot3(a, b, dims):
    def one(x, y):
        return lax.dot_general(x, y, (dims, ((), ())), preferred_element_type=F32)

    return one(a[0], b[0]) + (one(a[0], b[1]) + one(a[1], b[0]))


def place():
    position = lax.axis_index("fsdp")
    return lax.rem(lax.div(position, 2), 4), lax.rem(position, 2), lax.axis_index("rep")


def run_copies(pairs, sems):
    copies = [pltpu.make_async_copy(src, dst, sems.at[i]) for i, (src, dst) in enumerate(pairs)]
    for copy in copies:
        copy.start()
    for copy in copies:
        copy.wait()


def relay(hops, sems):
    n = len(hops)
    first = [pltpu.make_async_copy(src, mid, sems.at[i]) for i, (src, mid, _) in enumerate(hops)]
    second = [pltpu.make_async_copy(mid, dst, sems.at[n + i]) for i, (_, mid, dst) in enumerate(hops)]
    for copy in first:
        copy.start()
    for arrival, copy in zip(first, second):
        arrival.wait()
        copy.start()
    for copy in second:
        copy.wait()


def dma(n):
    return pltpu.SemaphoreType.DMA((n,))


def copies_of(pairs, sems):
    return [pltpu.make_async_copy(src, dst, sems.at[i]) for i, (src, dst) in enumerate(pairs)]


def deal(grad):
    width = len(BANDED) * BLOCK

    def kernel(grad, out, stage, sems):
        hops = []
        for owner in range(8):
            columns = pl.ds(owner * OWNED, width)
            hops.append((grad.at[:, columns], stage.at[owner], out.at[owner]))
        relay(hops, sems)

    return pl.pallas_call(
        kernel,
        name="deal",
        in_specs=[HBM],
        out_specs=HBM,
        out_shape=array(8, 64, width),
        scratch_shapes=[pltpu.VMEM((8, 64, width), F32), dma(16)],
        compiler_params=PARAMS,
        cost_estimate=cost(0, 4 << 20),
    )(grad)


def deal_core(grad):
    def kernel(grad, out, stage, sems):
        _, core, _ = place()
        hops = []
        for y in range(4):
            start = pl.multiple_of((2 * y + 1 - core) * OWNED + FILLED * BLOCK, BLOCK)
            hops.append((grad.at[:, pl.ds(start, BLOCK)], stage.at[y], out.at[y]))
        relay(hops, sems)

    return pl.pallas_call(
        kernel,
        name="deal_core",
        in_specs=[HBM],
        out_specs=HBM,
        out_shape=array(4, 64, BLOCK),
        scratch_shapes=[pltpu.VMEM((4, 64, BLOCK), F32), dma(8)],
        compiler_params=PARAMS,
        cost_estimate=cost(0, 1 << 20),
    )(grad)


def pack(grad, got):
    def kernel(grad, got, own, *rest):
        *outs, stage, sems = rest
        y, core, _ = place()
        hops = []
        for i, (shift, out) in enumerate(zip((0,) + SHIFTS, (own, *outs))):
            target = lax.rem(y + shift, 4)
            start = pl.multiple_of((2 * target + core) * OWNED + FILLED * BLOCK, BLOCK)
            hops.append((grad.at[:, pl.ds(start, BLOCK)], stage.at[2 * i], out.at[core]))
            hops.append((got.at[target], stage.at[2 * i + 1], out.at[1 - core]))
        relay(hops, sems)

    return pl.pallas_call(
        kernel,
        name="pack",
        in_specs=[HBM] * 2,
        out_specs=[HBM] * 4,
        out_shape=[array(2, 64, BLOCK)] * 4,
        scratch_shapes=[pltpu.VMEM((8, 64, BLOCK), F32), dma(16)],
        compiler_params=PARAMS,
        cost_estimate=cost(0, 2 << 20),
    )(grad, got)


def replicas():
    me = lax.axis_index("rep")
    return [lax.rem(me + i, 4) for i in range(4)]


def pack_roots(roots, picks, diagonals, after_this=None):
    waits = [] if after_this is None else [after_this]
    across_shape = [array(len(diagonals), BAND, BAND)] if diagonals else []

    def kernel(*refs):
        *outs, stage, extra, sems = refs[len(roots) + len(waits) :]
        me, after, facing, before = replicas()
        loads = [(refs[a].at[slot], stage.at[i]) for i, (a, slot) in enumerate(picks)]
        loads += [(refs[a].at[slot, :, at(me)], extra.at[i]) for i, (a, slot) in enumerate(diagonals)]
        run_copies(loads, sems)
        down, up = outs[:2]
        pairs = []
        for i in range(2):
            own = stage.at[i, :, at(me)]
            pairs += [(own, down.at[i]), (own, up.at[i])]
            pairs.append((stage.at[i, :, at(after)], down.at[2 + i]))
            pairs.append((stage.at[i, :, at(before)], up.at[2 + i]))
            pairs.append((stage.at[i, :, at(facing)], (down, up)[i].at[4]))
        if diagonals:
            pairs.append((extra, outs[2]))
        run_copies(pairs, sems)

    return pl.pallas_call(
        kernel,
        name="pack_roots",
        in_specs=[HBM] * (len(roots) + len(waits)),
        out_specs=[HBM] * (2 + len(across_shape)),
        out_shape=[array(5, BAND, BAND)] * 2 + across_shape,
        scratch_shapes=[pltpu.VMEM((2, BAND, BLOCK), F32), pltpu.VMEM((4, BAND, BAND), F32), dma(12)],
        compiler_params=PARAMS,
        cost_estimate=cost(0, 1 << 20),
    )(*roots, *waits)


def whole_roots(roots, picks, above, below, across, first, weight):
    def kernel(*refs):
        *roots, above_in, below_in, across_in, high, low, bands, above, below, across, whole, parts, sems = refs
        me, after, facing, before = replicas()
        pairs = [(roots[a].at[slot], bands.at[i]) for i, (a, slot) in enumerate(picks)]
        run_copies(pairs + [(above_in, above), (below_in, below), (across_in.at[pl.ds(first, 2)], across)], sems)
        stores = []

        def put(a, b, block):
            whole[at(a), at(b)] = block
            whole[at(b), at(a)] = block.T

        for i in range(2):
            whole[at(me), :] = bands[i]
            for other in (after, facing, before):
                whole[at(other), at(me)] = bands[i, :, at(other)].T
            whole[at(after), at(after)] = above[i]
            whole[at(before), at(before)] = below[i]
            whole[at(facing), at(facing)] = across[i]
            put(after, facing, above[2 + i])
            put(before, facing, below[2 + i])
            if i:
                put(before, after, below[4])
            else:
                put(after, before, above[4])
            parts[0, i], parts[1, i] = split(whole[...])
            for j, out in enumerate((high, low)):
                stores.append(pltpu.make_async_copy(parts.at[j, i], out.at[i], sems.at[5 + 2 * i + j]))
                stores[-1].start()
        for copy in stores:
            copy.wait()

    return pl.pallas_call(
        kernel,
        name="whole_roots",
        in_specs=[HBM] * (len(roots) + 3),
        out_specs=[HBM] * 2,
        out_shape=[array(2, BLOCK, BLOCK, dtype=BF16)] * 2,
        scratch_shapes=[
            pltpu.VMEM((2, BAND, BLOCK), F32),
            pltpu.VMEM((5, BAND, BAND), F32),
            pltpu.VMEM((5, BAND, BAND), F32),
            pltpu.VMEM((2, BAND, BAND), F32),
            pltpu.VMEM((BLOCK, BLOCK), F32),
            pltpu.VMEM((2, 2, BLOCK, BLOCK), BF16),
            dma(9),
        ],
        compiler_params=PARAMS,
        cost_estimate=pl.CostEstimate(flops=weight, bytes_accessed=4 << 20, transcendentals=0),
    )(*roots, above, below, across)


def apply_band(blocks, high, low, right_root):
    n = len(BANDED)

    def kernel(blocks, high, low, right, out, grad, parts, right_v, result, sems):
        loads = []
        for i, slot in enumerate(BANDED):
            pairs = [(blocks.at[:, pl.ds(i * BLOCK, BLOCK)], grad.at[i]), (right.at[slot], right_v.at[i])]
            pairs += [(high.at[i], parts.at[i, 0]), (low.at[i], parts.at[i, 1])]
            loads.append([pltpu.make_async_copy(a, b, sems.at[i, j]) for j, (a, b) in enumerate(pairs)])
            for copy in loads[-1]:
                copy.start()
        stores = []
        for i in range(n):
            for copy in loads[i]:
                copy.wait()
            half = dot_stacked(stacked(right_v[i]), split(grad[i]), ((1,), (1,)))
            columns = pl.ds(i * BAND, BAND)
            result[:, columns] = dot_stacked(stacked(half), (parts[i, 0], parts[i, 1]), ((1,), (0,))).T
            stores.append(pltpu.make_async_copy(result.at[:, columns], out.at[:, columns], sems.at[i, 4]))
            stores[-1].start()
        for copy in stores:
            copy.wait()

    return pl.pallas_call(
        kernel,
        name="apply_band",
        in_specs=[HBM] * 4,
        out_specs=HBM,
        out_shape=array(BLOCK, n * BAND),
        scratch_shapes=[
            pltpu.VMEM((n, BLOCK, BLOCK), F32),
            pltpu.VMEM((n, 2, BLOCK, BLOCK), BF16),
            pltpu.VMEM((n, BAND, BLOCK), F32),
            pltpu.VMEM((BLOCK, n * BAND), F32),
            pltpu.SemaphoreType.DMA((n, 5)),
        ],
        compiler_params=PARAMS,
        cost_estimate=cost(n * 12 * BLOCK * BLOCK * BAND, n * 3 << 20),
    )(blocks, high, low, right_root)


def row_pairs(pieces, grad):
    y, _, _ = place()
    pairs = []
    for shift, piece in zip((0,) + SHIFTS, pieces):
        source = lax.rem(y + 4 - shift, 4)
        for core in range(2):
            rows = pl.ds(pl.multiple_of(source * BAND + core * 64, 64), 64)
            pairs.append((piece.at[core], grad.at[rows, :]))
    return pairs


def apply_whole(pieces, high, low):
    def kernel(*refs):
        *pieces, high, low, out, grad, parts, result, sems = refs
        pairs = row_pairs(pieces, grad) + [(high, parts.at[0]), (low, parts.at[1])]
        run_copies(pairs, sems)
        half = dot3(split(grad[...]), (parts[0, 1], parts[1, 1]), ((1,), (0,)))
        result[...] = dot3((parts[0, 0], parts[1, 0]), split(half), ((1,), (0,)))
        run_copies([(result, out)], sems)

    return pl.pallas_call(
        kernel,
        name="apply_whole",
        in_specs=[HBM] * 6,
        out_specs=HBM,
        out_shape=array(BLOCK, BLOCK),
        scratch_shapes=[
            pltpu.VMEM((BLOCK, BLOCK), F32),
            pltpu.VMEM((2, 2, BLOCK, BLOCK), BF16),
            pltpu.VMEM((BLOCK, BLOCK), F32),
            dma(10),
        ],
        compiler_params=PARAMS,
        cost_estimate=cost(12 * BLOCK * BLOCK * BLOCK, 4 << 20),
    )(*pieces, high, low)


def grams(blocks, pieces, left_stat, right_stat):
    def kernel(blocks, *refs):
        *pieces, left, right, left_out, right_out, grad, stats, sems = refs
        me = lax.axis_index("rep")
        loads = []
        for slot in range(SLOTS):
            pairs = [(left.at[slot], stats.at[0, slot]), (right.at[slot], stats.at[1, slot])]
            if slot in BANDED:
                columns = pl.ds(BANDED.index(slot) * BLOCK, BLOCK)
                pairs.append((blocks.at[:, columns], grad.at[slot]))
            else:
                pairs += row_pairs(pieces, grad.at[slot])
            loads.append([pltpu.make_async_copy(a, b, sems.at[slot, i]) for i, (a, b) in enumerate(pairs)])
            for copy in loads[-1]:
                copy.start()
        stores = []
        weight = (1.0 - STAT_DECAY) / BLOCK
        for slot in range(SLOTS):
            for copy in loads[slot]:
                copy.wait()
            whole = split(grad[slot])
            rows = stacked(grad[slot, at(me), :])
            columns = stacked(grad[slot, :, at(me)].T)
            stats[0, slot] = STAT_DECAY * stats[0, slot] + weight * dot_stacked(rows, whole, ((1,), (1,)))
            stats[1, slot] = STAT_DECAY * stats[1, slot] + weight * dot_stacked(columns, whole, ((1,), (0,)))
            for i, out in enumerate((left_out, right_out)):
                stores.append(pltpu.make_async_copy(stats.at[i, slot], out.at[slot], sems.at[slot, 10 + i]))
                stores[-1].start()
        for copy in stores:
            copy.wait()

    return pl.pallas_call(
        kernel,
        name="grams",
        in_specs=[HBM] * 7,
        out_specs=[HBM] * 2,
        out_shape=[array(SLOTS, BAND, BLOCK)] * 2,
        scratch_shapes=[
            pltpu.VMEM((SLOTS, BLOCK, BLOCK), F32),
            pltpu.VMEM((2, SLOTS, BAND, BLOCK), F32),
            pltpu.SemaphoreType.DMA((SLOTS, 12)),
        ],
        compiler_params=PARAMS,
        cost_estimate=pl.CostEstimate(flops=1 << 37, bytes_accessed=7 << 20, transcendentals=0),
    )(blocks, *pieces, left_stat, right_stat)


def join_whole(blocks, out):
    def kernel(blocks, _, out, stage, sems):
        hops = []
        for owner in range(8):
            columns = pl.ds((SLOTS * owner + FILLED) * BLOCK, BLOCK)
            hops.append((blocks.at[owner], stage.at[owner], out.at[:, columns]))
        relay(hops, sems)

    return pl.pallas_call(
        kernel,
        name="join_whole",
        in_specs=[HBM] * 2,
        out_specs=HBM,
        out_shape=array(64, 8 * OWNED),
        scratch_shapes=[pltpu.VMEM((8, 64, BLOCK), F32), dma(16)],
        input_output_aliases={1: 0},
        compiler_params=PARAMS,
        cost_estimate=cost(0, 2 << 20),
    )(blocks, out)


def join_bands(pieces):
    n = len(BANDED)

    def kernel(*refs):
        *pieces, out, bands, rows, sems = refs
        me = replicas()
        loads = []
        for owner in range(8):
            pairs = [(piece.at[owner], bands.at[i, owner]) for i, piece in enumerate(pieces)]
            loads.append([pltpu.make_async_copy(a, b, sems.at[owner, i]) for i, (a, b) in enumerate(pairs)])
            for copy in loads[-1]:
                copy.start()
        stores = []
        for owner in range(8):
            for copy in loads[owner]:
                copy.wait()
            for j, slot in enumerate(BANDED):
                for i, shift in enumerate((0,) + SHIFTS):
                    band = bands[i, owner, :, j * BAND : (j + 1) * BAND]
                    rows[owner, :, at(j * REPLICAS + me[(REPLICAS - shift) % REPLICAS])] = band
                target = out.at[:, pl.ds((SLOTS * owner + slot) * BLOCK, BLOCK)]
                copy = pltpu.make_async_copy(rows.at[owner, :, pl.ds(j * BLOCK, BLOCK)], target, sems.at[owner, 4 + j])
                copy.start()
                stores.append(copy)
        for copy in stores:
            copy.wait()

    return pl.pallas_call(
        kernel,
        name="join_bands",
        in_specs=[HBM] * REPLICAS,
        out_specs=HBM,
        out_shape=array(64, 8 * OWNED),
        scratch_shapes=[
            pltpu.VMEM((REPLICAS, 8, 64, n * BAND), F32),
            pltpu.VMEM((8, 64, n * BLOCK), F32),
            pltpu.SemaphoreType.DMA((8, 4 + n)),
        ],
        compiler_params=PARAMS,
        cost_estimate=cost(0, n * 2 << 20),
    )(*pieces)


def shards(grad, left_stat, right_stat, left_root, right_root):
    groups = [[8 * g + p for p in range(8)] for g in range(8)]
    order = lax.optimization_barrier

    def exchange(x):
        return lax.all_to_all(x, "fsdp", 0, 0, axis_index_groups=groups, tiled=True)

    def along_y(x, distance):
        route = [(i, i - i % 8 + (i % 8 + 2 * distance) % 8) for i in range(64)]
        return lax.ppermute(x, "fsdp", route)

    def along_x(x, distance):
        return lax.ppermute(x, "rep", [(i, (i + distance) % REPLICAS) for i in range(REPLICAS)])

    def other_core(x):
        return lax.ppermute(x, "fsdp", [(i, i ^ 1) for i in range(64)])

    early, late = ((0, 0), (0, 1)), ((0, 2), (1, 2))
    roots = (left_root, right_root)
    dealt, roots = order((deal(grad), roots))
    blocks = exchange(dealt).reshape(BLOCK, len(BANDED) * BLOCK)
    down, up, across = pack_roots(roots, early, early + late)
    across = along_x(across, 2)
    first_whole = whole_roots(roots, early, along_x(down, 3), along_x(up, 1), across, 0, 0)
    down, up = pack_roots(roots, late, (), across)
    second_whole = whole_roots(roots, late, along_x(down, 3), along_x(up, 1), across, 2, 1 << 37)
    got = other_core(deal_core(grad))
    kept, *sent = pack(grad, got)
    pieces = [kept] + [along_y(x, d) for x, d in zip(sent, SHIFTS)]
    own = exchange(apply_band(blocks, *first_whole, right_root).reshape(8, 64, len(BANDED) * BAND))
    own, pieces = order((own, pieces))
    bands = [own] + [along_x(own, d) for d in SHIFTS]
    filled = exchange(apply_whole(pieces, *second_whole).reshape(8, 64, BLOCK))
    out = join_whole(filled, join_bands(bands))
    left_next, right_next = grams(blocks, pieces, left_stat, right_stat)
    return out, left_next, right_next


def solution(mesh):
    band = P("fsdp", "rep", None)
    return jax.shard_map(
        shards,
        mesh=mesh,
        in_specs=(P("fsdp", None), band, band, band, band),
        out_specs=(P("fsdp", None), band, band),
        check_vma=False,
    )
```

profile of v0, /device:TPU:1, one launch (start us, length us, event | category | flops | bytes accessed | tf_op | source)
XLA Modules:
  0.0 90.6 jit_solution(7047416559168048892)
XLA Ops:
  0.6 2.4 %deal.1 = f32[8,64,1024]{2,1,0:T(8,128)} custom-call(f32[64,12288]{1,0:T(8,128)} %grad.5), custom_call_target="tpu_custom_call" | custom-call | flops 1 | bytes 1 | tf_op jit(solution)/shard_map/deal/pallas_call | solution.py:105
  3.0 7.5 %all-to-all-start = ((f32[8,64,1024]{2,1,0:T(8,128)}), f32[8,64,1024]{2,1,0:T(8,128)}, u32[]{:S(2)}, u32[]{:S(2)}) async-start(f32[8,64,1024]{2,1,0:T(8,128)} %deal.1), calls=%async_computation | async-start | bytes 4194304 | tf_op jit(solution)/shard_map/all_to_all | solution.py:447
  10.5 2.1 %pack_roots.2 = (f32[5,128,128]{2,1,0:T(8,128)}, f32[5,128,128]{2,1,0:T(8,128)}, f32[4,128,128]{2,1,0:T(8,128)}) custom-call(f32[3,128,512]{2,1,0:T(8,128)} %refs_0_.3, f32[3,128,512]{2,1,0:T(8,128)} %refs_1_.3), custom_call_target="tpu_custom_call" | custom-call | flops 1 | bytes 1 | tf_op jit(solution)/shard_map/pack_roots/pallas_call | solution.py:189
  13.9 1.8 %deal_core.1 = f32[4,64,512]{2,1,0:T(8,128)} custom-call(f32[64,12288]{1,0:T(8,128)} %grad.5), custom_call_target="tpu_custom_call" | custom-call | flops 1 | bytes 1 | tf_op jit(solution)/shard_map/deal_core/pallas_call | solution.py:126
  17.6 4.6 %collective-permute-done.2.refs_4_.refs_2_ = f32[4,128,128]{2,1,0:T(8,128)S(1)} collective-permute-done((f32[4,128,128]{2,1,0:T(8,128)}, f32[4,128,128]{2,1,0:T(8,128)S(1)}, u32[]{:S(2)}, u32[]{:S(2)}) %collective-permute-start.2) | collective-permute-done | bytes 262176 | tf_op jit(solution)/shard_map/ppermute | solution.py:454
  22.8 2.0 %pack_roots.3 = (f32[5,128,128]{2,1,0:T(8,128)}, f32[5,128,128]{2,1,0:T(8,128)}) custom-call(f32[3,128,512]{2,1,0:T(8,128)} %refs_0_.3, f32[3,128,512]{2,1,0:T(8,128)} %refs_1_.3, f32[4,128,128]{2,1,0:T(8,128)} %copy-done), custom_call_target="tpu_custom_call" | custom-call | flops 1 | bytes 1 | tf_op jit(solution)/shard_map/pack_roots/pallas_call | solution.py:189
  26.4 1.7 %collective-permute-done.refs_2_ = f32[5,128,128]{2,1,0:T(8,128)} collective-permute-done((f32[5,128,128]{2,1,0:T(8,128)}, f32[5,128,128]{2,1,0:T(8,128)}, u32[]{:S(2)}, u32[]{:S(2)}) %collective-permute-start) | collective-permute-done | bytes 327712 | tf_op jit(solution)/shard_map/ppermute | solution.py:454
  28.1 1.7 %collective-permute-done.1.refs_3_ = f32[5,128,128]{2,1,0:T(8,128)} collective-permute-done((f32[5,128,128]{2,1,0:T(8,128)}, f32[5,128,128]{2,1,0:T(8,128)}, u32[]{:S(2)}, u32[]{:S(2)}) %collective-permute-start.1) | collective-permute-done | bytes 327712 | tf_op jit(solution)/shard_map/ppermute | solution.py:454
  29.7 3.3 %whole_roots.2 = (bf16[2,512,512]{2,1,0:T(8,128)(2,1)}, bf16[2,512,512]{2,1,0:T(8,128)(2,1)}) custom-call(f32[3,128,512]{2,1,0:T(8,128)} %refs_0_.3, f32[3,128,512]{2,1,0:T(8,128)} %refs_1_.3, f32[5,128,128]{2,1,0:T(8,128)} %collective-permute-done.refs_2_, f32[5,128,128]{2,1,0:T(8,128)} %collective-permute-done.1.refs_3_, f32[4,128,128]{2,1,0:T(8,128)} %copy-done), custom_call_target="tpu_custom_call" | custom-call | bytes 4194304 | tf_op jit(solution)/shard_map/whole_roots/pallas_call | solution.py:233
  33.0 2.1 %pack.1 = (f32[2,64,512]{2,1,0:T(8,128)}, f32[2,64,512]{2,1,0:T(8,128)}, f32[2,64,512]{2,1,0:T(8,128)}, f32[2,64,512]{2,1,0:T(8,128)}) custom-call(f32[64,12288]{1,0:T(8,128)} %grad.5, f32[4,64,512]{2,1,0:T(8,128)} %collective-permute-done.3.got), custom_call_target="tpu_custom_call" | custom-call | flops 1 | bytes 1 | tf_op jit(solution)/shard_map/pack/pallas_call | solution.py:150
  35.1 1.4 %collective-permute-start.4 = (f32[2,64,512]{2,1,0:T(8,128)}, f32[2,64,512]{2,1,0:T(8,128)S(1)}, u32[]{:S(2)}, u32[]{:S(2)}) collective-permute-start(f32[2,64,512]{2,1,0:T(8,128)} %get-tuple-element.35), channel_id=1, source_target_pairs={{0,8},{4,12},{8,16},{12,20},{16,24},{20,28},{24,0},{28,4},{32,40},... | collective-permute-start | bytes 786440 | tf_op jit(solution)/shard_map/ppermute | solution.py:451
  36.5 1.4 %collective-permute-start.5 = (f32[2,64,512]{2,1,0:T(8,128)}, f32[2,64,512]{2,1,0:T(8,128)}, u32[]{:S(2)}, u32[]{:S(2)}) collective-permute-start(f32[2,64,512]{2,1,0:T(8,128)} %get-tuple-element.36), channel_id=1, source_target_pairs={{0,24},{4,28},{8,0},{12,4},{16,8},{20,12},{24,16},{28,20},{32,56},... | collective-permute-start | bytes 786440 | tf_op jit(solution)/shard_map/ppermute | solution.py:451
  37.9 1.6 %collective-permute-start.6 = (f32[2,64,512]{2,1,0:T(8,128)}, f32[2,64,512]{2,1,0:T(8,128)}, u32[]{:S(2)}, u32[]{:S(2)}) collective-permute-start(f32[2,64,512]{2,1,0:T(8,128)} %get-tuple-element.37), channel_id=1, source_target_pairs={{0,16},{4,20},{8,24},{12,28},{16,0},{20,4},{24,8},{28,12},{32,48},... | collective-permute-start | bytes 786440 | tf_op jit(solution)/shard_map/ppermute | solution.py:451
  39.5 4.1 %apply_band.1 = f32[512,256]{1,0:T(8,128)} custom-call(f32[512,1024]{1,0:T(8,128)} %bitcast.blocks, bf16[2,512,512]{2,1,0:T(8,128)(2,1)} %get-tuple-element.32.high, bf16[2,512,512]{2,1,0:T(8,128)(2,1)} %get-tuple-element.33.low, f32[3,128,512]{2,1,0:T(8,128)} %refs_1_.3), custom_call_target="tpu_custom_call" | custom-call | flops 1 | bytes 1 | tf_op jit(solution)/shard_map/apply_band/pallas_call | solution.py:276
  43.6 5.5 %all-to-all-start.1 = ((f32[8,64,256]{2,1,0:T(8,128)}), f32[8,64,256]{2,1,0:T(8,128)}, u32[]{:S(2)}, u32[]{:S(2)}) async-start(f32[8,64,256]{2,1,0:T(8,128)} %bitcast.4), calls=%async_computation.1 | async-start | bytes 1048576 | tf_op jit(solution)/shard_map/all_to_all | solution.py:447
  49.1 3.3 %whole_roots.3 = (bf16[2,512,512]{2,1,0:T(8,128)(2,1)}, bf16[2,512,512]{2,1,0:T(8,128)(2,1)}) custom-call(f32[3,128,512]{2,1,0:T(8,128)} %refs_0_.3, f32[3,128,512]{2,1,0:T(8,128)} %refs_1_.3, f32[5,128,128]{2,1,0:T(8,128)} %collective-permute-done.7.refs_2_, f32[5,128,128]{2,1,0:T(8,128)} %collective-permute-done.8.refs_3_, f32[4,128,128]{2,1,0:T(8,128)} %copy-done), custom_call_target="tpu_custom_call" | custom-call | flops 137438953472 | bytes 4194304 | tf_op jit(solution)/shard_map/whole_roots/pallas_call | solution.py:233
  52.4 6.3 %all-to-all-done.1.refs_0_ = f32[8,64,256]{2,1,0:T(8,128)} async-done(((f32[8,64,256]{2,1,0:T(8,128)}), f32[8,64,256]{2,1,0:T(8,128)}, u32[]{:S(2)}, u32[]{:S(2)}) %all-to-all-start.1) | async-done | bytes 524320 | tf_op jit(solution)/shard_map/all_to_all | solution.py:447
  61.4 4.9 %apply_whole.1 = f32[512,512]{1,0:T(8,128)} custom-call(f32[2,64,512]{2,1,0:T(8,128)} %get-tuple-element.38.refs_0_, f32[2,64,512]{2,1,0:T(8,128)} %copy-done.1, f32[2,64,512]{2,1,0:T(8,128)} %collective-permute-done.5.refs_2_, f32[2,64,512]{2,1,0:T(8,128)} %collective-permute-done.6.refs_3_, bf16[2,512,512]{2,1,0:T(8,128)(2,1)} %get-tuple-element.44.refs_4_, ...), custom_call_target="tpu_custom_call" | custom-call | flops 1 | bytes 1 | tf_op jit(solution)/shard_map/apply_whole/pallas_call | solution.py:314
  66.4 5.8 %all-to-all-start.2 = ((f32[8,64,512]{2,1,0:T(8,128)}), f32[8,64,512]{2,1,0:T(8,128)}, u32[]{:S(2)}, u32[]{:S(2)}) async-start(f32[8,64,512]{2,1,0:T(8,128)} %bitcast.3), calls=%async_computation.2 | async-start | bytes 2097152 | tf_op jit(solution)/shard_map/all_to_all | solution.py:447
  72.2 4.6 %grams.1 = (f32[3,128,512]{2,1,0:T(8,128)}, f32[3,128,512]{2,1,0:T(8,128)}) custom-call(f32[512,1024]{1,0:T(8,128)} %bitcast.blocks, f32[2,64,512]{2,1,0:T(8,128)} %get-tuple-element.38.refs_0_, f32[2,64,512]{2,1,0:T(8,128)} %copy-done.1, f32[2,64,512]{2,1,0:T(8,128)} %collective-permute-done.5.refs_2_, f32[2,64,512]{2,1,0:T(8,128)} %collective-permute-done.6.refs_3_, ...), custom_call_target="tpu_custom_call" | custom-call | flops 137438953472 | bytes 7340032 | tf_op jit(solution)/shard_map/grams/pallas_call | solution.py:362
  76.8 6.5 %collective-permute-done.10.refs_2_ = f32[8,64,256]{2,1,0:T(8,128)} collective-permute-done((f32[8,64,256]{2,1,0:T(8,128)}, f32[8,64,256]{2,1,0:T(8,128)}, u32[]{:S(2)}, u32[]{:S(2)}) %collective-permute-start.10) | collective-permute-done | bytes 524320 | tf_op jit(solution)/shard_map/ppermute | solution.py:454
  83.2 2.3 %collective-permute-done.9.refs_1_ = f32[8,64,256]{2,1,0:T(8,128)} collective-permute-done((f32[8,64,256]{2,1,0:T(8,128)}, f32[8,64,256]{2,1,0:T(8,128)}, u32[]{:S(2)}, u32[]{:S(2)}) %collective-permute-start.9) | collective-permute-done | bytes 524320 | tf_op jit(solution)/shard_map/ppermute | solution.py:454
  85.6 2.7 %join_bands.1._ = f32[64,12288]{1,0:T(8,128)} custom-call(f32[8,64,256]{2,1,0:T(8,128)} %all-to-all-done.1.refs_0_, f32[8,64,256]{2,1,0:T(8,128)} %collective-permute-done.9.refs_1_, f32[8,64,256]{2,1,0:T(8,128)} %collective-permute-done.10.refs_2_, f32[8,64,256]{2,1,0:T(8,128)} %collective-permute-done.11.refs_3_), custom_call_target="tpu_custom_call" | custom-call | flops 1 | bytes 1 | tf_op jit(solution)/shard_map/join_bands/pallas_call | solution.py:426
  88.3 2.1 %join_whole.1 = f32[64,12288]{1,0:T(8,128)} custom-call(f32[8,64,512]{2,1,0:T(8,128)} %all-to-all-done.2.blocks, f32[64,12288]{1,0:T(8,128)} %join_bands.1._), custom_call_target="tpu_custom_call", output_to_operand_aliasing={{}: (1, {})} | custom-call | flops 1 | bytes 1 | tf_op jit(solution)/shard_map/join_whole/pallas_call | solution.py:386
  (22 shorter events, 8.2 us)
Async XLA Ops:
  3.0 36.5 %all-to-all-start = ((f32[8,64,1024]{2,1,0:T(8,128)}), f32[8,64,1024]{2,1,0:T(8,128)}, u32[]{:S(2)}, u32[]{:S(2)}) async-start(f32[8,64,1024]{2,1,0:T(8,128)} %deal.1), calls=%async_computation | async-start | bytes 4194304 | tf_op jit(solution)/shard_map/all_to_all | solution.py:447
  12.6 9.6 %collective-permute-start.2 = (f32[4,128,128]{2,1,0:T(8,128)}, f32[4,128,128]{2,1,0:T(8,128)S(1)}, u32[]{:S(2)}, u32[]{:S(2)}) collective-permute-start(f32[4,128,128]{2,1,0:T(8,128)} %get-tuple-element.31), channel_id=1, source_target_pairs={{0,2},{1,3},{2,0},{3,1},{4,6},{5,7},{6,4},{7,5},{8,10},{9,11},{10,... | collective-permute-start | bytes 786440 | tf_op jit(solution)/shard_map/ppermute | solution.py:454
  15.7 17.3 %collective-permute-start.3 = (f32[4,64,512]{2,1,0:T(8,128)}, f32[4,64,512]{2,1,0:T(8,128)}, u32[]{:S(2)}, u32[]{:S(2)}) collective-permute-start(f32[4,64,512]{2,1,0:T(8,128)} %deal_core.1), channel_id=1, source_target_pairs={{0,4},{4,0},{8,12},{12,8},{16,20},{20,16},{24,28},{28,24},{32,36},... | collective-permute-start | bytes 1572872 | tf_op jit(solution)/shard_map/ppermute | solution.py:457
  16.1 12.0 %collective-permute-start = (f32[5,128,128]{2,1,0:T(8,128)}, f32[5,128,128]{2,1,0:T(8,128)}, u32[]{:S(2)}, u32[]{:S(2)}) collective-permute-start(f32[5,128,128]{2,1,0:T(8,128)} %get-tuple-element.29), channel_id=1, source_target_pairs={{0,3},{1,0},{2,1},{3,2},{4,7},{5,4},{6,5},{7,6},{8,11},{9,8},{10,9... | collective-permute-start | bytes 983048 | tf_op jit(solution)/shard_map/ppermute | solution.py:454
  17.0 12.7 %collective-permute-start.1 = (f32[5,128,128]{2,1,0:T(8,128)}, f32[5,128,128]{2,1,0:T(8,128)}, u32[]{:S(2)}, u32[]{:S(2)}) collective-permute-start(f32[5,128,128]{2,1,0:T(8,128)} %get-tuple-element.30), channel_id=1, source_target_pairs={{0,1},{1,2},{2,3},{3,0},{4,5},{5,6},{6,7},{7,4},{8,9},{9,10},{10,1... | collective-permute-start | bytes 983048 | tf_op jit(solution)/shard_map/ppermute | solution.py:454
  22.1 0.7 copy-start
  24.8 24.3 %collective-permute-start.7 = (f32[5,128,128]{2,1,0:T(8,128)}, f32[5,128,128]{2,1,0:T(8,128)}, u32[]{:S(2)}, u32[]{:S(2)}) collective-permute-start(f32[5,128,128]{2,1,0:T(8,128)} %get-tuple-element.42), channel_id=1, source_target_pairs={{0,3},{1,0},{2,1},{3,2},{4,7},{5,4},{6,5},{7,6},{8,11},{9,8},{10,9... | collective-permute-start | bytes 983048 | tf_op jit(solution)/shard_map/ppermute | solution.py:454
  26.1 23.0 %collective-permute-start.8 = (f32[5,128,128]{2,1,0:T(8,128)}, f32[5,128,128]{2,1,0:T(8,128)}, u32[]{:S(2)}, u32[]{:S(2)}) collective-permute-start(f32[5,128,128]{2,1,0:T(8,128)} %get-tuple-element.43), channel_id=1, source_target_pairs={{0,1},{1,2},{2,3},{3,0},{4,5},{5,6},{6,7},{7,4},{8,9},{9,10},{10,1... | collective-permute-start | bytes 983048 | tf_op jit(solution)/shard_map/ppermute | solution.py:454
  35.1 17.2 %collective-permute-start.4 = (f32[2,64,512]{2,1,0:T(8,128)}, f32[2,64,512]{2,1,0:T(8,128)S(1)}, u32[]{:S(2)}, u32[]{:S(2)}) collective-permute-start(f32[2,64,512]{2,1,0:T(8,128)} %get-tuple-element.35), channel_id=1, source_target_pairs={{0,8},{4,12},{8,16},{12,20},{16,24},{20,28},{24,0},{28,4},{32,40},... | collective-permute-start | bytes 786440 | tf_op jit(solution)/shard_map/ppermute | solution.py:451
  36.5 15.9 %collective-permute-start.5 = (f32[2,64,512]{2,1,0:T(8,128)}, f32[2,64,512]{2,1,0:T(8,128)}, u32[]{:S(2)}, u32[]{:S(2)}) collective-permute-start(f32[2,64,512]{2,1,0:T(8,128)} %get-tuple-element.36), channel_id=1, source_target_pairs={{0,24},{4,28},{8,0},{12,4},{16,8},{20,12},{24,16},{28,20},{32,56},... | collective-permute-start | bytes 786440 | tf_op jit(solution)/shard_map/ppermute | solution.py:451
  37.9 14.5 %collective-permute-start.6 = (f32[2,64,512]{2,1,0:T(8,128)}, f32[2,64,512]{2,1,0:T(8,128)}, u32[]{:S(2)}, u32[]{:S(2)}) collective-permute-start(f32[2,64,512]{2,1,0:T(8,128)} %get-tuple-element.37), channel_id=1, source_target_pairs={{0,16},{4,20},{8,24},{12,28},{16,0},{20,4},{24,8},{28,12},{32,48},... | collective-permute-start | bytes 786440 | tf_op jit(solution)/shard_map/ppermute | solution.py:451
  43.6 15.1 %all-to-all-start.1 = ((f32[8,64,256]{2,1,0:T(8,128)}), f32[8,64,256]{2,1,0:T(8,128)}, u32[]{:S(2)}, u32[]{:S(2)}) async-start(f32[8,64,256]{2,1,0:T(8,128)} %bitcast.4), calls=%async_computation.1 | async-start | bytes 1048576 | tf_op jit(solution)/shard_map/all_to_all | solution.py:447
  52.4 9.1 %copy-start.1 = (f32[2,64,512]{2,1,0:T(8,128)}, f32[2,64,512]{2,1,0:T(8,128)S(1)}, u32[]{:S(2)}) copy-start(f32[2,64,512]{2,1,0:T(8,128)S(1)} %collective-permute-done.4.refs_1_) | copy-start | bytes 786436
  58.7 18.1 %collective-permute-start.11 = (f32[8,64,256]{2,1,0:T(8,128)}, f32[8,64,256]{2,1,0:T(8,128)}, u32[]{:S(2)}, u32[]{:S(2)}) collective-permute-start(f32[8,64,256]{2,1,0:T(8,128)} %all-to-all-done.1.refs_0_), channel_id=1, source_target_pairs={{0,2},{1,3},{2,0},{3,1},{4,6},{5,7},{6,4},{7,5},{8,10},{9,11},{10,... | collective-permute-start | bytes 1572872 | tf_op jit(solution)/shard_map/ppermute | solution.py:454
  60.0 23.3 %collective-permute-start.10 = (f32[8,64,256]{2,1,0:T(8,128)}, f32[8,64,256]{2,1,0:T(8,128)}, u32[]{:S(2)}, u32[]{:S(2)}) collective-permute-start(f32[8,64,256]{2,1,0:T(8,128)} %all-to-all-done.1.refs_0_), channel_id=1, source_target_pairs={{0,3},{1,0},{2,1},{3,2},{4,7},{5,4},{6,5},{7,6},{8,11},{9,8},{10,9... | collective-permute-start | bytes 1572872 | tf_op jit(solution)/shard_map/ppermute | solution.py:454
  61.2 24.4 %collective-permute-start.9 = (f32[8,64,256]{2,1,0:T(8,128)}, f32[8,64,256]{2,1,0:T(8,128)}, u32[]{:S(2)}, u32[]{:S(2)}) collective-permute-start(f32[8,64,256]{2,1,0:T(8,128)} %all-to-all-done.1.refs_0_), channel_id=1, source_target_pairs={{0,1},{1,2},{2,3},{3,0},{4,5},{5,6},{6,7},{7,4},{8,9},{9,10},{10,1... | collective-permute-start | bytes 1572872 | tf_op jit(solution)/shard_map/ppermute | solution.py:454
  66.4 21.9 %all-to-all-start.2 = ((f32[8,64,512]{2,1,0:T(8,128)}), f32[8,64,512]{2,1,0:T(8,128)}, u32[]{:S(2)}, u32[]{:S(2)}) async-start(f32[8,64,512]{2,1,0:T(8,128)} %bitcast.3), calls=%async_computation.2 | async-start | bytes 2097152 | tf_op jit(solution)/shard_map/all_to_all | solution.py:447
where the time goes:
time: 91.1 us; the launch traced here: 90.6 us
  Pallas kernels  35.3 us (39%)
  starting transfers between devices  30.6 us (34%)
  waiting for transfers between devices  23 us (25%)
  between operations  0.95 us (1%)
    all_to_all x3, starting transfers between devices, exchange(): return lax.all_to_all(x, 'fsdp', 0, 0, axis_index_groups=groups, tiled=True)  18.8 us
    ppermute x8, waiting for transfers between devices, along_x(): lax.ppermute(x, 'rep', [(i, (i + distance) % REPLICAS) for i in range(REP...  16.7 us
    ppermute x8, starting transfers between devices, along_x(): lax.ppermute(x, 'rep', [(i, (i + distance) % REPLICAS) for i in range(REP...  7.11 us
    pallas_call x2, Pallas kernels, whole_roots(): pl.pallas_call(kernel, name='whole_roots', in_specs=[HBM] * (len(roots) +...  6.54 us
    all_to_all x3, waiting for transfers between devices, exchange(): return lax.all_to_all(x, 'fsdp', 0, 0, axis_index_groups=groups, tiled=True)  6.28 us
    pallas_call x1, Pallas kernels, apply_whole(): pl.pallas_call(kernel, name='apply_whole', in_specs=[HBM] * 6, out_specs=...  4.91 us
    pallas_call x1, Pallas kernels, grams(): pl.pallas_call(kernel, name='grams', in_specs=[HBM] * 7, out_specs=[HBM]...  4.56 us
    ppermute x3, starting transfers between devices, along_y(): return lax.ppermute(x, 'fsdp', route)  4.35 us
  transfers between devices with their start and end apart: 15, of which 6 were waited for; matrix products, arithmetic and copies ran while one was open for 0% of the time, Pallas kernels for 34%

commit v1 on v0

--- a/solution.py
+++ b/solution.py
@@ -198,77 +198,64 @@
     )(*roots, *waits)
 
 
-def whole_roots(roots, picks, above, below, across, first, weight):
+def assemble(i, bands, above, below, across, whole):
+    me, after, facing, before = replicas()
+
+    def put(a, b, block):
+        whole[at(a), at(b)] = block
+        whole[at(b), at(a)] = block.T
+
+    whole[at(me), :] = bands[i]
+    for other in (after, facing, before):
+        whole[at(other), at(me)] = bands[i, :, at(other)].T
+    whole[at(after), at(after)] = above[i]
+    whole[at(before), at(before)] = below[i]
+    whole[at(facing), at(facing)] = across[i]
+    put(after, facing, above[2 + i])
+    put(before, facing, below[2 + i])
+    if i:
+        put(before, after, below[4])
+    else:
+        put(after, before, above[4])
+
+
+def root_scratch():
+    return [
+        pltpu.VMEM((2, BAND, BLOCK), F32),
+        pltpu.VMEM((5, BAND, BAND), F32),
+        pltpu.VMEM((5, BAND, BAND), F32),
+        pltpu.VMEM((2, BAND, BAND), F32),
+        pltpu.VMEM((BLOCK, BLOCK), F32),
+    ]
+
+
+def apply_band(blocks, roots, picks, above, below, across, first):
+    n = len(BANDED)
+
     def kernel(*refs):
-        *roots, above_in, below_in, across_in, high, low, bands, above, below, across, whole, parts, sems = refs
-        me, after, facing, before = replicas()
-        pairs = [(roots[a].at[slot], bands.at[i]) for i, (a, slot) in enumerate(picks)]
-        run_copies(pairs + [(above_in, above), (below_in, below), (across_in.at[pl.ds(first, 2)], across)], sems)
-        stores = []
-
-        def put(a, b, block):
-            whole[at(a), at(b)] = block
-            whole[at(b), at(a)] = block.T
-
-        for i in range(2):
-            whole[at(me), :] = bands[i]
-            for other in (after, facing, before):
-                whole[at(other), at(me)] = bands[i, :, at(other)].T
-            whole[at(after), at(after)] = above[i]
-            whole[at(before), at(before)] = below[i]
-            whole[at(facing), at(facing)] = across[i]
-            put(after, facing, above[2 + i])
-            put(before, facing, below[2 + i])
-            if i:
-                put(before, after, below[4])
-            else:
-                put(after, before, above[4])
-            parts[0, i], parts[1, i] = split(whole[...])
-            for j, out in enumerate((high, low)):
-                stores.append(pltpu.make_async_copy(parts.at[j, i], out.at[i], sems.at[5 + 2 * i + j]))
-                stores[-1].start()
-        for copy in stores:
+        blocks, left, right, above_in, below_in, across_in, out = refs[:7]
+        bands, above, below, across, whole, grad, right_v, result, sems = refs[7:]
+        pairs = [(left.at[slot], bands.at[i]) for i, (_, slot) in enumerate(picks)]
+        pairs += [(above_in, above), (below_in, below), (across_in.at[pl.ds(first, 2)], across)]
+        pairs += [(right.at[slot], right_v.at[i]) for i, slot in enumerate(BANDED)]
+        copies = copies_of(pairs, sems)
+        loads = [
+            pltpu.make_async_copy(blocks.at[:, pl.ds(i * BLOCK, BLOCK)], grad.at[i], sems.at[len(pairs) + i])
+            for i in range(n)
+        ]
+        for copy in copies + loads:
+            copy.start()
+        for copy in copies:
             copy.wait()
-
-    return pl.pallas_call(
-        kernel,
-        name="whole_roots",
-        in_specs=[HBM] * (len(roots) + 3),
-        out_specs=[HBM] * 2,
-        out_shape=[array(2, BLOCK, BLOCK, dtype=BF16)] * 2,
-        scratch_shapes=[
-            pltpu.VMEM((2, BAND, BLOCK), F32),
-            pltpu.VMEM((5, BAND, BAND), F32),
-            pltpu.VMEM((5, BAND, BAND), F32),
-            pltpu.VMEM((2, BAND, BAND), F32),
-            pltpu.VMEM((BLOCK, BLOCK), F32),
-            pltpu.VMEM((2, 2, BLOCK, BLOCK), BF16),
-            dma(9),
-        ],
-        compiler_params=PARAMS,
-        cost_estimate=pl.CostEstimate(flops=weight, bytes_accessed=4 << 20, transcendentals=0),
-    )(*roots, above, below, across)
-
-
-def apply_band(blocks, high, low, right_root):
-    n = len(BANDED)
-
-    def kernel(blocks, high, low, right, out, grad, parts, right_v, result, sems):
-        loads = []
-        for i, slot in enumerate(BANDED):
-            pairs = [(blocks.at[:, pl.ds(i * BLOCK, BLOCK)], grad.at[i]), (right.at[slot], right_v.at[i])]
-            pairs += [(high.at[i], parts.at[i, 0]), (low.at[i], parts.at[i, 1])]
-            loads.append([pltpu.make_async_copy(a, b, sems.at[i, j]) for j, (a, b) in enumerate(pairs)])
-            for copy in loads[-1]:
-                copy.start()
         stores = []
         for i in range(n):
-            for copy in loads[i]:
-                copy.wait()
+            assemble(i, bands, above, below, across, whole)
+            left_root = split(whole[...])
+            loads[i].wait()
             half = dot_stacked(stacked(right_v[i]), split(grad[i]), ((1,), (1,)))
             columns = pl.ds(i * BAND, BAND)
-            result[:, columns] = dot_stacked(stacked(half), (parts[i, 0], parts[i, 1]), ((1,), (0,))).T
-            stores.append(pltpu.make_async_copy(result.at[:, columns], out.at[:, columns], sems.at[i, 4]))
+            result[:, columns] = dot_stacked(stacked(half), left_root, ((1,), (0,))).T
+            stores.append(pltpu.make_async_copy(result.at[:, columns], out.at[:, columns], sems.at[i]))
             stores[-1].start()
         for copy in stores:
             copy.wait()
@@ -276,19 +263,19 @@
     return pl.pallas_call(
         kernel,
         name="apply_band",
-        in_specs=[HBM] * 4,
+        in_specs=[HBM] * 6,
         out_specs=HBM,
         out_shape=array(BLOCK, n * BAND),
-        scratch_shapes=[
+        scratch_shapes=root_scratch()
+        + [
             pltpu.VMEM((n, BLOCK, BLOCK), F32),
-            pltpu.VMEM((n, 2, BLOCK, BLOCK), BF16),
             pltpu.VMEM((n, BAND, BLOCK), F32),
             pltpu.VMEM((BLOCK, n * BAND), F32),
-            pltpu.SemaphoreType.DMA((n, 5)),
+            dma(9),
         ],
         compiler_params=PARAMS,
         cost_estimate=cost(n * 12 * BLOCK * BLOCK * BAND, n * 3 << 20),
-    )(blocks, high, low, right_root)
+    )(blocks, *roots, above, below, across)
 
 
 def row_pairs(pieces, grad):
@@ -302,30 +289,36 @@
     return pairs
 
 
-def apply_whole(pieces, high, low):
+def apply_whole(pieces, roots, picks, above, below, across, first):
     def kernel(*refs):
-        *pieces, high, low, out, grad, parts, result, sems = refs
-        pairs = row_pairs(pieces, grad) + [(high, parts.at[0]), (low, parts.at[1])]
-        run_copies(pairs, sems)
-        half = dot3(split(grad[...]), (parts[0, 1], parts[1, 1]), ((1,), (0,)))
-        result[...] = dot3((parts[0, 0], parts[1, 0]), split(half), ((1,), (0,)))
-        run_copies([(result, out)], sems)
+        pieces, refs = refs[:4], refs[4:]
+        *roots, above_in, below_in, across_in, out, bands, above, below, across, whole, grad, result, sems = refs
+        pairs = [(roots[a].at[slot], bands.at[i]) for i, (a, slot) in enumerate(picks)]
+        pairs += [(above_in, above), (below_in, below), (across_in.at[pl.ds(first, 2)], across)]
+        run_copies(pairs + row_pairs(pieces, grad), sems)
+        assemble(1, bands, above, below, across, whole)
+        half = split(dot3(split(grad[...]), split(whole[...]), ((1,), (0,))))
+        assemble(0, bands, above, below, across, whole)
+        stores = []
+        for i in range(4):
+            rows = pl.ds(i * BAND, BAND)
+            result[rows, :] = dot_stacked(stacked(whole[rows, :]), half, ((1,), (0,)))
+            stores.append(pltpu.make_async_copy(result.at[rows, :], out.at[rows, :], sems.at[i]))
+            stores[-1].start()
+        for copy in stores:
+            copy.wait()
 
     return pl.pallas_call(
         kernel,
         name="apply_whole",
-        in_specs=[HBM] * 6,
+        in_specs=[HBM] * (7 + len(roots)),
         out_specs=HBM,
         out_shape=array(BLOCK, BLOCK),
-        scratch_shapes=[
-            pltpu.VMEM((BLOCK, BLOCK), F32),
-            pltpu.VMEM((2, 2, BLOCK, BLOCK), BF16),
-            pltpu.VMEM((BLOCK, BLOCK), F32),
-            dma(10),
-        ],
-        compiler_params=PARAMS,
-        cost_estimate=cost(12 * BLOCK * BLOCK * BLOCK, 4 << 20),
-    )(*pieces, high, low)
+        scratch_shapes=root_scratch()
+        + [pltpu.VMEM((BLOCK, BLOCK), F32), pltpu.VMEM((BLOCK, BLOCK), F32), dma(13)],
+        compiler_params=PARAMS,
+        cost_estimate=pl.CostEstimate(flops=1 << 37, bytes_accessed=4 << 20, transcendentals=0),
+    )(*pieces, *roots, above, below, across)
 
 
 def grams(blocks, pieces, left_stat, right_stat):
@@ -375,36 +368,16 @@
     )(blocks, *pieces, left_stat, right_stat)
 
 
-def join_whole(blocks, out):
-    def kernel(blocks, _, out, stage, sems):
-        hops = []
-        for owner in range(8):
-            columns = pl.ds((SLOTS * owner + FILLED) * BLOCK, BLOCK)
-            hops.append((blocks.at[owner], stage.at[owner], out.at[:, columns]))
-        relay(hops, sems)
-
-    return pl.pallas_call(
-        kernel,
-        name="join_whole",
-        in_specs=[HBM] * 2,
-        out_specs=HBM,
-        out_shape=array(64, 8 * OWNED),
-        scratch_shapes=[pltpu.VMEM((8, 64, BLOCK), F32), dma(16)],
-        input_output_aliases={1: 0},
-        compiler_params=PARAMS,
-        cost_estimate=cost(0, 2 << 20),
-    )(blocks, out)
-
-
-def join_bands(pieces):
+def join(pieces, filled):
     n = len(BANDED)
 
     def kernel(*refs):
-        *pieces, out, bands, rows, sems = refs
+        *pieces, filled, out, bands, blocks, rows, sems = refs
         me = replicas()
         loads = []
         for owner in range(8):
             pairs = [(piece.at[owner], bands.at[i, owner]) for i, piece in enumerate(pieces)]
+            pairs.append((filled.at[owner], blocks.at[owner]))
             loads.append([pltpu.make_async_copy(a, b, sems.at[owner, i]) for i, (a, b) in enumerate(pairs)])
             for copy in loads[-1]:
                 copy.start()
@@ -416,27 +389,29 @@
                 for i, shift in enumerate((0,) + SHIFTS):
                     band = bands[i, owner, :, j * BAND : (j + 1) * BAND]
                     rows[owner, :, at(j * REPLICAS + me[(REPLICAS - shift) % REPLICAS])] = band
+            targets = [(rows.at[owner, :, pl.ds(j * BLOCK, BLOCK)], slot) for j, slot in enumerate(BANDED)]
+            for j, (source, slot) in enumerate(targets + [(blocks.at[owner], FILLED)]):
                 target = out.at[:, pl.ds((SLOTS * owner + slot) * BLOCK, BLOCK)]
-                copy = pltpu.make_async_copy(rows.at[owner, :, pl.ds(j * BLOCK, BLOCK)], target, sems.at[owner, 4 + j])
-                copy.start()
-                stores.append(copy)
+                stores.append(pltpu.make_async_copy(source, target, sems.at[owner, REPLICAS + 1 + j]))
+                stores[-1].start()
         for copy in stores:
             copy.wait()
 
     return pl.pallas_call(
         kernel,
-        name="join_bands",
-        in_specs=[HBM] * REPLICAS,
+        name="join",
+        in_specs=[HBM] * (REPLICAS + 1),
         out_specs=HBM,
         out_shape=array(64, 8 * OWNED),
         scratch_shapes=[
             pltpu.VMEM((REPLICAS, 8, 64, n * BAND), F32),
+            pltpu.VMEM((8, 64, BLOCK), F32),
             pltpu.VMEM((8, 64, n * BLOCK), F32),
-            pltpu.SemaphoreType.DMA((8, 4 + n)),
+            pltpu.SemaphoreType.DMA((8, REPLICAS + 1 + SLOTS)),
         ],
         compiler_params=PARAMS,
-        cost_estimate=cost(0, n * 2 << 20),
-    )(*pieces)
+        cost_estimate=cost(0, 6 << 20),
+    )(*pieces, filled)
 
 
 def shards(grad, left_stat, right_stat, left_root, right_root):
@@ -462,17 +437,18 @@
     blocks = exchange(dealt).reshape(BLOCK, len(BANDED) * BLOCK)
     down, up, across = pack_roots(roots, early, early + late)
     across = along_x(across, 2)
-    first_whole = whole_roots(roots, early, along_x(down, 3), along_x(up, 1), across, 0, 0)
-    down, up = pack_roots(roots, late, (), across)
-    second_whole = whole_roots(roots, late, along_x(down, 3), along_x(up, 1), across, 2, 1 << 37)
-    got = other_core(deal_core(grad))
-    kept, *sent = pack(grad, got)
+    second = pack_roots(roots, late, (), across)
+    kept, *sent = pack(grad, other_core(deal_core(grad)))
+    first = along_x(down, 3), along_x(up, 1)
+    second = along_x(second[0], 3), along_x(second[1], 1)
+    banded = apply_band(blocks, roots, early, *first, across, 0)
     pieces = [kept] + [along_y(x, d) for x, d in zip(sent, SHIFTS)]
-    own = exchange(apply_band(blocks, *first_whole, right_root).reshape(8, 64, len(BANDED) * BAND))
-    own, pieces = order((own, pieces))
+    own = exchange(banded.reshape(8, 64, len(BANDED) * BAND))
+    filled = apply_whole(pieces, roots, late, *second, across, 2)
+    own, filled = order((own, filled))
     bands = [own] + [along_x(own, d) for d in SHIFTS]
-    filled = exchange(apply_whole(pieces, *second_whole).reshape(8, 64, BLOCK))
-    out = join_whole(filled, join_bands(bands))
+    filled = exchange(filled.reshape(8, 64, BLOCK))
+    out = join(bands, filled)
     left_next, right_next = grams(blocks, pieces, left_stat, right_stat)
     return out, left_next, right_next
 

time: 91.1 us -> 87.4 us (0.959)
  Pallas kernels: 35.3 us -> 27.5 us
  waiting for transfers between devices: 23 us -> 26.7 us
    pallas_call x6 -> x3, Pallas kernels: 20.4 us -> 12.5 us  [the longest x1 4.66 us: apply_whole(): pl.pallas_call(kernel, name='apply_whole', in_specs=[HBM] * (7 + len(root...]
    ppermute x8, waiting for transfers between devices: 16.7 us -> 20.5 us  [along_x(): lax.ppermute(x, 'rep', [(i, (i + distance) % REPLICAS) for i in range(REP...]
  transfers between devices with their start and end apart: 15 -> 15, of which waited for: 6 -> 7; matrix products, arithmetic and copies ran while one was open for 0% -> 0% of each run, Pallas kernels for 34% -> 25%
where the time goes in v1:
time: 87.4 us; the launch traced here: 86.9 us
  starting transfers between devices  30.7 us (35%)
  Pallas kernels  27.5 us (31%)
  waiting for transfers between devices  26.7 us (31%)
  local copies, waits for them, and re-layouts  1.09 us (1%)
  between operations  0.9 us (1%)
    ppermute x8, waiting for transfers between devices, along_x(): lax.ppermute(x, 'rep', [(i, (i + distance) % REPLICAS) for i in range(REP...  20.5 us
    all_to_all x3, starting transfers between devices, exchange(): return lax.all_to_all(x, 'fsdp', 0, 0, axis_index_groups=groups, tiled=True)  18.7 us
    ppermute x8, starting transfers between devices, along_x(): lax.ppermute(x, 'rep', [(i, (i + distance) % REPLICAS) for i in range(REP...  6.91 us
    all_to_all x3, waiting for transfers between devices, exchange(): return lax.all_to_all(x, 'fsdp', 0, 0, axis_index_groups=groups, tiled=True)  5.9 us
    ppermute x3, starting transfers between devices, along_y(): return lax.ppermute(x, 'fsdp', route)  4.89 us
    pallas_call x1, Pallas kernels, apply_whole(): pl.pallas_call(kernel, name='apply_whole', in_specs=[HBM] * (7 + len(root...  4.66 us
    pallas_call x1, Pallas kernels, grams(): pl.pallas_call(kernel, name='grams', in_specs=[HBM] * 7, out_specs=[HBM]...  4.57 us
    pallas_call x1, Pallas kernels, apply_band(): pl.pallas_call(kernel, name='apply_band', in_specs=[HBM] * 6, out_specs=H...  4.55 us
  transfers between devices with their start and end apart: 15, of which 7 were waited for; matrix products, arithmetic and copies ran while one was open for 0% of the time, Pallas kernels for 25%

profile of v1, /device:TPU:1, one launch (start us, length us, event | category | flops | bytes accessed | tf_op | source)
XLA Modules:
  0.0 86.9 jit_solution(17113265963828207788)
XLA Ops:
  0.6 2.4 %deal.1 = f32[8,64,1024]{2,1,0:T(8,128)} custom-call(f32[64,12288]{1,0:T(8,128)} %grad.5), custom_call_target="tpu_custom_call" | custom-call | flops 1 | bytes 1 | tf_op jit(solution)/shard_map/deal/pallas_call | solution.py:105
  3.0 7.5 %all-to-all-start = ((f32[8,64,1024]{2,1,0:T(8,128)}), f32[8,64,1024]{2,1,0:T(8,128)}, u32[]{:S(2)}, u32[]{:S(2)}) async-start(f32[8,64,1024]{2,1,0:T(8,128)} %deal.1), calls=%async_computation | async-start | bytes 4194304 | tf_op jit(solution)/shard_map/all_to_all | solution.py:422
  10.5 1.8 %deal_core.1 = f32[4,64,512]{2,1,0:T(8,128)} custom-call(f32[64,12288]{1,0:T(8,128)} %grad.5), custom_call_target="tpu_custom_call" | custom-call | flops 1 | bytes 1 | tf_op jit(solution)/shard_map/deal_core/pallas_call | solution.py:126
  12.6 2.1 %pack_roots.2 = (f32[5,128,128]{2,1,0:T(8,128)}, f32[5,128,128]{2,1,0:T(8,128)}, f32[4,128,128]{2,1,0:T(8,128)}) custom-call(f32[3,128,512]{2,1,0:T(8,128)} %refs_4_.1, f32[3,128,512]{2,1,0:T(8,128)} %refs_5_.1), custom_call_target="tpu_custom_call" | custom-call | flops 1 | bytes 1 | tf_op jit(solution)/shard_map/pack_roots/pallas_call | solution.py:189
  14.7 1.2 %collective-permute-start.2 = (f32[4,128,128]{2,1,0:T(8,128)}, f32[4,128,128]{2,1,0:T(8,128)S(1)}, u32[]{:S(2)}, u32[]{:S(2)}) collective-permute-start(f32[4,128,128]{2,1,0:T(8,128)} %get-tuple-element.24), channel_id=1, source_target_pairs={{0,2},{1,3},{2,0},{3,1},{4,6},{5,7},{6,4},{7,5},{8,10},{9,11},{10,... | collective-permute-start | bytes 786440 | tf_op jit(solution)/shard_map/ppermute | solution.py:429
  15.9 0.9 %collective-permute-start = (f32[5,128,128]{2,1,0:T(8,128)}, f32[5,128,128]{2,1,0:T(8,128)}, u32[]{:S(2)}, u32[]{:S(2)}) collective-permute-start(f32[5,128,128]{2,1,0:T(8,128)} %get-tuple-element.22), channel_id=1, source_target_pairs={{0,3},{1,0},{2,1},{3,2},{4,7},{5,4},{6,5},{7,6},{8,11},{9,8},{10,9... | collective-permute-start | bytes 983048 | tf_op jit(solution)/shard_map/ppermute | solution.py:429
  17.4 6.7 %collective-permute-done.2.refs_5_.refs_2_.refs_8_ = f32[4,128,128]{2,1,0:T(8,128)S(1)} collective-permute-done((f32[4,128,128]{2,1,0:T(8,128)}, f32[4,128,128]{2,1,0:T(8,128)S(1)}, u32[]{:S(2)}, u32[]{:S(2)}) %collective-permute-start.2) | collective-permute-done | bytes 262176 | tf_op jit(solution)/shard_map/ppermute | solution.py:429
  24.8 2.0 %pack_roots.3 = (f32[5,128,128]{2,1,0:T(8,128)}, f32[5,128,128]{2,1,0:T(8,128)}) custom-call(f32[3,128,512]{2,1,0:T(8,128)} %refs_4_.1, f32[3,128,512]{2,1,0:T(8,128)} %refs_5_.1, f32[4,128,128]{2,1,0:T(8,128)} %copy-done), custom_call_target="tpu_custom_call" | custom-call | flops 1 | bytes 1 | tf_op jit(solution)/shard_map/pack_roots/pallas_call | solution.py:189
  28.3 2.1 %pack.1 = (f32[2,64,512]{2,1,0:T(8,128)}, f32[2,64,512]{2,1,0:T(8,128)}, f32[2,64,512]{2,1,0:T(8,128)}, f32[2,64,512]{2,1,0:T(8,128)}) custom-call(f32[64,12288]{1,0:T(8,128)} %grad.5, f32[4,64,512]{2,1,0:T(8,128)} %collective-permute-done.3.got), custom_call_target="tpu_custom_call" | custom-call | flops 1 | bytes 1 | tf_op jit(solution)/shard_map/pack/pallas_call | solution.py:150
  30.4 1.9 %collective-permute-start.4 = (f32[2,64,512]{2,1,0:T(8,128)}, f32[2,64,512]{2,1,0:T(8,128)}, u32[]{:S(2)}, u32[]{:S(2)}) collective-permute-start(f32[2,64,512]{2,1,0:T(8,128)} %get-tuple-element.26), channel_id=1, source_target_pairs={{0,8},{4,12},{8,16},{12,20},{16,24},{20,28},{24,0},{28,4},{32,40},... | collective-permute-start | bytes 786440 | tf_op jit(solution)/shard_map/ppermute | solution.py:426
  32.3 1.3 %collective-permute-start.5 = (f32[2,64,512]{2,1,0:T(8,128)}, f32[2,64,512]{2,1,0:T(8,128)}, u32[]{:S(2)}, u32[]{:S(2)}) collective-permute-start(f32[2,64,512]{2,1,0:T(8,128)} %get-tuple-element.27), channel_id=1, source_target_pairs={{0,24},{4,28},{8,0},{12,4},{16,8},{20,12},{24,16},{28,20},{32,56},... | collective-permute-start | bytes 786440 | tf_op jit(solution)/shard_map/ppermute | solution.py:426
  33.7 1.6 %collective-permute-start.6 = (f32[2,64,512]{2,1,0:T(8,128)}, f32[2,64,512]{2,1,0:T(8,128)}, u32[]{:S(2)}, u32[]{:S(2)}) collective-permute-start(f32[2,64,512]{2,1,0:T(8,128)} %get-tuple-element.28), channel_id=1, source_target_pairs={{0,16},{4,20},{8,24},{12,28},{16,0},{20,4},{24,8},{28,12},{32,48},... | collective-permute-start | bytes 786440 | tf_op jit(solution)/shard_map/ppermute | solution.py:426
  35.3 1.7 %all-to-all-done = f32[8,64,1024]{2,1,0:T(8,128)} async-done(((f32[8,64,1024]{2,1,0:T(8,128)}), f32[8,64,1024]{2,1,0:T(8,128)}, u32[]{:S(2)}, u32[]{:S(2)}) %all-to-all-start) | async-done | bytes 2097184 | tf_op jit(solution)/shard_map/all_to_all | solution.py:422
  37.0 4.5 %apply_band.1 = f32[512,256]{1,0:T(8,128)} custom-call(f32[512,1024]{1,0:T(8,128)} %bitcast.refs_0_.blocks, f32[3,128,512]{2,1,0:T(8,128)} %refs_4_.1, f32[3,128,512]{2,1,0:T(8,128)} %refs_5_.1, f32[5,128,128]{2,1,0:T(8,128)} %collective-permute-done.refs_3_, f32[5,128,128]{2,1,0:T(8,128)} %collective-permute-done.1.refs_4_, f32[4,128,128]{2,1,0:T(8,128)} %copy-done), custom_call_target="tpu_custom_call" | custom-call | flops 1 | bytes 1 | tf_op jit(solution)/shard_map/apply_band/pallas_call | solution.py:263
  41.6 5.4 %all-to-all-start.1 = ((f32[8,64,256]{2,1,0:T(8,128)}), f32[8,64,256]{2,1,0:T(8,128)}, u32[]{:S(2)}, u32[]{:S(2)}) async-start(f32[8,64,256]{2,1,0:T(8,128)} %bitcast.3), calls=%async_computation.1 | async-start | bytes 1048576 | tf_op jit(solution)/shard_map/all_to_all | solution.py:422
  47.7 4.7 %apply_whole.1 = f32[512,512]{1,0:T(8,128)} custom-call(f32[2,64,512]{2,1,0:T(8,128)} %get-tuple-element.25.refs_0_, f32[2,64,512]{2,1,0:T(8,128)} %collective-permute-done.4.refs_1_, f32[2,64,512]{2,1,0:T(8,128)} %collective-permute-done.5.refs_2_, f32[2,64,512]{2,1,0:T(8,128)} %collective-permute-done.6.refs_3_, f32[3,128,512]{2,1,0:T(8,128)} %refs_4_.1, ...), custom_call_target="tpu_custom_call" | custom-call | flops 137438953472 | bytes 4194304 | tf_op jit(solution)/shard_map/apply_whole/pallas_call | solution.py:311
  52.3 4.2 %all-to-all-done.1.refs_0_ = f32[8,64,256]{2,1,0:T(8,128)} async-done(((f32[8,64,256]{2,1,0:T(8,128)}), f32[8,64,256]{2,1,0:T(8,128)}, u32[]{:S(2)}, u32[]{:S(2)}) %all-to-all-start.1) | async-done | bytes 524320 | tf_op jit(solution)/shard_map/all_to_all | solution.py:422
  56.5 1.2 %collective-permute-start.11 = (f32[8,64,256]{2,1,0:T(8,128)}, f32[8,64,256]{2,1,0:T(8,128)}, u32[]{:S(2)}, u32[]{:S(2)}) collective-permute-start(f32[8,64,256]{2,1,0:T(8,128)} %all-to-all-done.1.refs_0_), channel_id=1, source_target_pairs={{0,2},{1,3},{2,0},{3,1},{4,6},{5,7},{6,4},{7,5},{8,10},{9,11},{10,... | collective-permute-start | bytes 1572872 | tf_op jit(solution)/shard_map/ppermute | solution.py:429
  59.2 5.8 %all-to-all-start.2 = ((f32[8,64,512]{2,1,0:T(8,128)}), f32[8,64,512]{2,1,0:T(8,128)}, u32[]{:S(2)}, u32[]{:S(2)}) async-start(f32[8,64,512]{2,1,0:T(8,128)} %bitcast.4), calls=%async_computation.2 | async-start | bytes 2097152 | tf_op jit(solution)/shard_map/all_to_all | solution.py:422
  65.0 4.6 %grams.1 = (f32[3,128,512]{2,1,0:T(8,128)}, f32[3,128,512]{2,1,0:T(8,128)}) custom-call(f32[512,1024]{1,0:T(8,128)} %bitcast.refs_0_.blocks, f32[2,64,512]{2,1,0:T(8,128)} %get-tuple-element.25.refs_0_, f32[2,64,512]{2,1,0:T(8,128)} %collective-permute-done.4.refs_1_, f32[2,64,512]{2,1,0:T(8,128)} %collective-permute-done.5.refs_2_, ...), custom_call_target="tpu_custom_call" | custom-call | flops 137438953472 | bytes 7340032 | tf_op jit(solution)/shard_map/grams/pallas_call | solution.py:355
  69.6 1.3 %collective-permute-done.11.refs_3_ = f32[8,64,256]{2,1,0:T(8,128)} collective-permute-done((f32[8,64,256]{2,1,0:T(8,128)}, f32[8,64,256]{2,1,0:T(8,128)}, u32[]{:S(2)}, u32[]{:S(2)}) %collective-permute-start.11) | collective-permute-done | bytes 524320 | tf_op jit(solution)/shard_map/ppermute | solution.py:429
  71.0 11.0 %collective-permute-done.10.refs_2_ = f32[8,64,256]{2,1,0:T(8,128)} collective-permute-done((f32[8,64,256]{2,1,0:T(8,128)}, f32[8,64,256]{2,1,0:T(8,128)}, u32[]{:S(2)}, u32[]{:S(2)}) %collective-permute-start.10) | collective-permute-done | bytes 524320 | tf_op jit(solution)/shard_map/ppermute | solution.py:429
  81.9 1.5 %collective-permute-done.9.refs_1_ = f32[8,64,256]{2,1,0:T(8,128)} collective-permute-done((f32[8,64,256]{2,1,0:T(8,128)}, f32[8,64,256]{2,1,0:T(8,128)}, u32[]{:S(2)}, u32[]{:S(2)}) %collective-permute-start.9) | collective-permute-done | bytes 524320 | tf_op jit(solution)/shard_map/ppermute | solution.py:429
  83.4 3.3 %join.1 = f32[64,12288]{1,0:T(8,128)} custom-call(f32[8,64,256]{2,1,0:T(8,128)} %all-to-all-done.1.refs_0_, f32[8,64,256]{2,1,0:T(8,128)} %collective-permute-done.9.refs_1_, f32[8,64,256]{2,1,0:T(8,128)} %collective-permute-done.10.refs_2_, f32[8,64,256]{2,1,0:T(8,128)} %collective-permute-done.11.refs_3_, f32[8,64,512]{2,1,0:T(8,128)} %all-to-all-done.2.refs_4_), custom_call_target="tpu_custom_call" | custom-call | flops 1 | bytes 1 | tf_op jit(solution)/shard_map/join/pallas_call | solution.py:400
  (19 shorter events, 5.2 us)
Async XLA Ops:
  3.0 34.0 %all-to-all-start = ((f32[8,64,1024]{2,1,0:T(8,128)}), f32[8,64,1024]{2,1,0:T(8,128)}, u32[]{:S(2)}, u32[]{:S(2)}) async-start(f32[8,64,1024]{2,1,0:T(8,128)} %deal.1), calls=%async_computation | async-start | bytes 4194304 | tf_op jit(solution)/shard_map/all_to_all | solution.py:422
  12.3 16.0 %collective-permute-start.3 = (f32[4,64,512]{2,1,0:T(8,128)}, f32[4,64,512]{2,1,0:T(8,128)}, u32[]{:S(2)}, u32[]{:S(2)}) collective-permute-start(f32[4,64,512]{2,1,0:T(8,128)} %deal_core.1), channel_id=1, source_target_pairs={{0,4},{4,0},{8,12},{12,8},{16,20},{20,16},{24,28},{28,24},{32,36},... | collective-permute-start | bytes 1572872 | tf_op jit(solution)/shard_map/ppermute | solution.py:432
  14.7 9.4 %collective-permute-start.2 = (f32[4,128,128]{2,1,0:T(8,128)}, f32[4,128,128]{2,1,0:T(8,128)S(1)}, u32[]{:S(2)}, u32[]{:S(2)}) collective-permute-start(f32[4,128,128]{2,1,0:T(8,128)} %get-tuple-element.24), channel_id=1, source_target_pairs={{0,2},{1,3},{2,0},{3,1},{4,6},{5,7},{6,4},{7,5},{8,10},{9,11},{10,... | collective-permute-start | bytes 786440 | tf_op jit(solution)/shard_map/ppermute | solution.py:429
  15.9 16.4 %collective-permute-start = (f32[5,128,128]{2,1,0:T(8,128)}, f32[5,128,128]{2,1,0:T(8,128)}, u32[]{:S(2)}, u32[]{:S(2)}) collective-permute-start(f32[5,128,128]{2,1,0:T(8,128)} %get-tuple-element.22), channel_id=1, source_target_pairs={{0,3},{1,0},{2,1},{3,2},{4,7},{5,4},{6,5},{7,6},{8,11},{9,8},{10,9... | collective-permute-start | bytes 983048 | tf_op jit(solution)/shard_map/ppermute | solution.py:429
  16.8 16.9 %collective-permute-start.1 = (f32[5,128,128]{2,1,0:T(8,128)}, f32[5,128,128]{2,1,0:T(8,128)}, u32[]{:S(2)}, u32[]{:S(2)}) collective-permute-start(f32[5,128,128]{2,1,0:T(8,128)} %get-tuple-element.23), channel_id=1, source_target_pairs={{0,1},{1,2},{2,3},{3,0},{4,5},{5,6},{6,7},{7,4},{8,9},{9,10},{10,1... | collective-permute-start | bytes 983048 | tf_op jit(solution)/shard_map/ppermute | solution.py:429
  24.0 0.7 copy-start
  26.8 20.2 %collective-permute-start.7 = (f32[5,128,128]{2,1,0:T(8,128)}, f32[5,128,128]{2,1,0:T(8,128)S(1)}, u32[]{:S(2)}, u32[]{:S(2)}) collective-permute-start(f32[5,128,128]{2,1,0:T(8,128)} %get-tuple-element.29), channel_id=1, source_target_pairs={{0,3},{1,0},{2,1},{3,2},{4,7},{5,4},{6,5},{7,6},{8,11},{9,8},{10,9... | collective-permute-start | bytes 983048 | tf_op jit(solution)/shard_map/ppermute | solution.py:429
  27.6 19.4 %collective-permute-start.8 = (f32[5,128,128]{2,1,0:T(8,128)}, f32[5,128,128]{2,1,0:T(8,128)}, u32[]{:S(2)}, u32[]{:S(2)}) collective-permute-start(f32[5,128,128]{2,1,0:T(8,128)} %get-tuple-element.30), channel_id=1, source_target_pairs={{0,1},{1,2},{2,3},{3,0},{4,5},{5,6},{6,7},{7,4},{8,9},{9,10},{10,1... | collective-permute-start | bytes 983048 | tf_op jit(solution)/shard_map/ppermute | solution.py:429
  30.4 16.5 %collective-permute-start.4 = (f32[2,64,512]{2,1,0:T(8,128)}, f32[2,64,512]{2,1,0:T(8,128)}, u32[]{:S(2)}, u32[]{:S(2)}) collective-permute-start(f32[2,64,512]{2,1,0:T(8,128)} %get-tuple-element.26), channel_id=1, source_target_pairs={{0,8},{4,12},{8,16},{12,20},{16,24},{20,28},{24,0},{28,4},{32,40},... | collective-permute-start | bytes 786440 | tf_op jit(solution)/shard_map/ppermute | solution.py:426
  32.3 14.6 %collective-permute-start.5 = (f32[2,64,512]{2,1,0:T(8,128)}, f32[2,64,512]{2,1,0:T(8,128)}, u32[]{:S(2)}, u32[]{:S(2)}) collective-permute-start(f32[2,64,512]{2,1,0:T(8,128)} %get-tuple-element.27), channel_id=1, source_target_pairs={{0,24},{4,28},{8,0},{12,4},{16,8},{20,12},{24,16},{28,20},{32,56},... | collective-permute-start | bytes 786440 | tf_op jit(solution)/shard_map/ppermute | solution.py:426
  33.7 13.6 %collective-permute-start.6 = (f32[2,64,512]{2,1,0:T(8,128)}, f32[2,64,512]{2,1,0:T(8,128)}, u32[]{:S(2)}, u32[]{:S(2)}) collective-permute-start(f32[2,64,512]{2,1,0:T(8,128)} %get-tuple-element.28), channel_id=1, source_target_pairs={{0,16},{4,20},{8,24},{12,28},{16,0},{20,4},{24,8},{28,12},{32,48},... | collective-permute-start | bytes 786440 | tf_op jit(solution)/shard_map/ppermute | solution.py:426
  41.6 15.0 %all-to-all-start.1 = ((f32[8,64,256]{2,1,0:T(8,128)}), f32[8,64,256]{2,1,0:T(8,128)}, u32[]{:S(2)}, u32[]{:S(2)}) async-start(f32[8,64,256]{2,1,0:T(8,128)} %bitcast.3), calls=%async_computation.1 | async-start | bytes 1048576 | tf_op jit(solution)/shard_map/all_to_all | solution.py:422
  46.9 0.7 copy-start.1
  56.5 14.4 %collective-permute-start.11 = (f32[8,64,256]{2,1,0:T(8,128)}, f32[8,64,256]{2,1,0:T(8,128)}, u32[]{:S(2)}, u32[]{:S(2)}) collective-permute-start(f32[8,64,256]{2,1,0:T(8,128)} %all-to-all-done.1.refs_0_), channel_id=1, source_target_pairs={{0,2},{1,3},{2,0},{3,1},{4,6},{5,7},{6,4},{7,5},{8,10},{9,11},{10,... | collective-permute-start | bytes 1572872 | tf_op jit(solution)/shard_map/ppermute | solution.py:429
  57.7 24.2 %collective-permute-start.10 = (f32[8,64,256]{2,1,0:T(8,128)}, f32[8,64,256]{2,1,0:T(8,128)}, u32[]{:S(2)}, u32[]{:S(2)}) collective-permute-start(f32[8,64,256]{2,1,0:T(8,128)} %all-to-all-done.1.refs_0_), channel_id=1, source_target_pairs={{0,3},{1,0},{2,1},{3,2},{4,7},{5,4},{6,5},{7,6},{8,11},{9,8},{10,9... | collective-permute-start | bytes 1572872 | tf_op jit(solution)/shard_map/ppermute | solution.py:429
  58.6 24.8 %collective-permute-start.9 = (f32[8,64,256]{2,1,0:T(8,128)}, f32[8,64,256]{2,1,0:T(8,128)}, u32[]{:S(2)}, u32[]{:S(2)}) collective-permute-start(f32[8,64,256]{2,1,0:T(8,128)} %all-to-all-done.1.refs_0_), channel_id=1, source_target_pairs={{0,1},{1,2},{2,3},{3,0},{4,5},{5,6},{6,7},{7,4},{8,9},{9,10},{10,1... | collective-permute-start | bytes 1572872 | tf_op jit(solution)/shard_map/ppermute | solution.py:429
  59.2 24.2 %all-to-all-start.2 = ((f32[8,64,512]{2,1,0:T(8,128)}), f32[8,64,512]{2,1,0:T(8,128)}, u32[]{:S(2)}, u32[]{:S(2)}) async-start(f32[8,64,512]{2,1,0:T(8,128)} %bitcast.4), calls=%async_computation.2 | async-start | bytes 2097152 | tf_op jit(solution)/shard_map/all_to_all | solution.py:422

commit v2 on v1

--- a/solution.py
+++ b/solution.py
@@ -164,38 +164,47 @@
     return [lax.rem(me + i, 4) for i in range(4)]
 
 
-def pack_roots(roots, picks, diagonals, after_this=None):
-    waits = [] if after_this is None else [after_this]
-    across_shape = [array(len(diagonals), BAND, BAND)] if diagonals else []
-
+def pack_roots(roots, picks):
     def kernel(*refs):
-        *outs, stage, extra, sems = refs[len(roots) + len(waits) :]
+        *outs, stage, sems = refs[len(roots) :]
         me, after, facing, before = replicas()
-        loads = [(refs[a].at[slot], stage.at[i]) for i, (a, slot) in enumerate(picks)]
-        loads += [(refs[a].at[slot, :, at(me)], extra.at[i]) for i, (a, slot) in enumerate(diagonals)]
-        run_copies(loads, sems)
-        down, up = outs[:2]
+        run_copies([(refs[a].at[slot], stage.at[i]) for i, (a, slot) in enumerate(picks)], sems)
         pairs = []
-        for i in range(2):
+        for i in range(4):
+            down, up = outs[1 + i // 2 * 2 : 3 + i // 2 * 2]
             own = stage.at[i, :, at(me)]
-            pairs += [(own, down.at[i]), (own, up.at[i])]
-            pairs.append((stage.at[i, :, at(after)], down.at[2 + i]))
-            pairs.append((stage.at[i, :, at(before)], up.at[2 + i]))
-            pairs.append((stage.at[i, :, at(facing)], (down, up)[i].at[4]))
-        if diagonals:
-            pairs.append((extra, outs[2]))
+            pairs += [(own, outs[0].at[i]), (own, down.at[i % 2]), (own, up.at[i % 2])]
+            pairs.append((stage.at[i, :, at(after)], down.at[2 + i % 2]))
+            pairs.append((stage.at[i, :, at(before)], up.at[2 + i % 2]))
+            pairs.append((stage.at[i, :, at(facing)], (down, up)[i % 2].at[4]))
         run_copies(pairs, sems)
 
     return pl.pallas_call(
         kernel,
         name="pack_roots",
-        in_specs=[HBM] * (len(roots) + len(waits)),
-        out_specs=[HBM] * (2 + len(across_shape)),
-        out_shape=[array(5, BAND, BAND)] * 2 + across_shape,
-        scratch_shapes=[pltpu.VMEM((2, BAND, BLOCK), F32), pltpu.VMEM((4, BAND, BAND), F32), dma(12)],
-        compiler_params=PARAMS,
-        cost_estimate=cost(0, 1 << 20),
-    )(*roots, *waits)
+        in_specs=[HBM] * len(roots),
+        out_specs=[HBM] * 5,
+        out_shape=[array(4, BAND, BAND)] + [array(5, BAND, BAND)] * 4,
+        scratch_shapes=[pltpu.VMEM((4, BAND, BLOCK), F32), dma(24)],
+        compiler_params=PARAMS,
+        cost_estimate=cost(0, 2 << 20),
+    )(*roots)
+
+
+def follow(x, earlier):
+    def kernel(*refs):
+        pass
+
+    return pl.pallas_call(
+        kernel,
+        name="follow",
+        in_specs=[HBM] * 2,
+        out_specs=HBM,
+        out_shape=array(*x.shape),
+        input_output_aliases={0: 0},
+        compiler_params=PARAMS,
+        cost_estimate=cost(0, 0),
+    )(x, earlier)
 
 
 def assemble(i, bands, above, below, across, whole):
@@ -364,7 +373,7 @@
             pltpu.SemaphoreType.DMA((SLOTS, 12)),
         ],
         compiler_params=PARAMS,
-        cost_estimate=pl.CostEstimate(flops=1 << 37, bytes_accessed=7 << 20, transcendentals=0),
+        cost_estimate=cost(36 * BLOCK * BLOCK * BAND, 7 << 20),
     )(blocks, *pieces, left_stat, right_stat)
 
 
@@ -373,7 +382,8 @@
 
     def kernel(*refs):
         *pieces, filled, out, bands, blocks, rows, sems = refs
-        me = replicas()
+        _, core, me = place()
+        sources = [me, lax.rem(me + 3 - 2 * core, 4), lax.rem(me + 1 + 2 * core, 4), lax.rem(me + 2, 4)]
         loads = []
         for owner in range(8):
             pairs = [(piece.at[owner], bands.at[i, owner]) for i, piece in enumerate(pieces)]
@@ -386,9 +396,8 @@
             for copy in loads[owner]:
                 copy.wait()
             for j, slot in enumerate(BANDED):
-                for i, shift in enumerate((0,) + SHIFTS):
-                    band = bands[i, owner, :, j * BAND : (j + 1) * BAND]
-                    rows[owner, :, at(j * REPLICAS + me[(REPLICAS - shift) % REPLICAS])] = band
+                for i, source in enumerate(sources):
+                    rows[owner, :, at(j * REPLICAS + source)] = bands[i, owner, :, j * BAND : (j + 1) * BAND]
             targets = [(rows.at[owner, :, pl.ds(j * BLOCK, BLOCK)], slot) for j, slot in enumerate(BANDED)]
             for j, (source, slot) in enumerate(targets + [(blocks.at[owner], FILLED)]):
                 target = out.at[:, pl.ds((SLOTS * owner + slot) * BLOCK, BLOCK)]
@@ -428,6 +437,10 @@
     def along_x(x, distance):
         return lax.ppermute(x, "rep", [(i, (i + distance) % REPLICAS) for i in range(REPLICAS)])
 
+    def around(x, direction):
+        ends = [(i, r, (r + (1 - 2 * (i % 2)) * direction) % REPLICAS) for i in range(64) for r in range(REPLICAS)]
+        return lax.ppermute(x, ("fsdp", "rep"), [(REPLICAS * i + r, REPLICAS * i + t) for i, r, t in ends])
+
     def other_core(x):
         return lax.ppermute(x, "fsdp", [(i, i ^ 1) for i in range(64)])
 
@@ -435,21 +448,20 @@
     roots = (left_root, right_root)
     dealt, roots = order((deal(grad), roots))
     blocks = exchange(dealt).reshape(BLOCK, len(BANDED) * BLOCK)
-    down, up, across = pack_roots(roots, early, early + late)
+    across, *first, down, up = pack_roots(roots, early + late)
     across = along_x(across, 2)
-    second = pack_roots(roots, late, (), across)
+    first = along_x(first[0], 3), along_x(first[1], 1)
     kept, *sent = pack(grad, other_core(deal_core(grad)))
-    first = along_x(down, 3), along_x(up, 1)
-    second = along_x(second[0], 3), along_x(second[1], 1)
+    second = along_x(follow(down, across), 3), along_x(follow(up, across), 1)
     banded = apply_band(blocks, roots, early, *first, across, 0)
     pieces = [kept] + [along_y(x, d) for x, d in zip(sent, SHIFTS)]
     own = exchange(banded.reshape(8, 64, len(BANDED) * BAND))
     filled = apply_whole(pieces, roots, late, *second, across, 2)
     own, filled = order((own, filled))
-    bands = [own] + [along_x(own, d) for d in SHIFTS]
+    near = around(own, 1)
     filled = exchange(filled.reshape(8, 64, BLOCK))
-    out = join(bands, filled)
     left_next, right_next = grams(blocks, pieces, left_stat, right_stat)
+    out = join([own, near, around(own, -1), around(near, 1)], filled)
     return out, left_next, right_next
 
 

time: 87.4 us -> 81.3 us (0.930)
  waiting for transfers between devices: 26.7 us -> 21.5 us
  Pallas kernels: 27.5 us -> 25.9 us
  starting transfers between devices: 30.7 us -> 31.9 us
    ppermute x8 -> x5, waiting for transfers between devices: 20.5 us -> 6.71 us  [along_x(): lax.ppermute(x, 'rep', [(i, (i + distance) % REPLICAS) for i in range(REP...]
    ppermute x0 -> x3, waiting for transfers between devices: none -> 4.8 us  [around(): lax.ppermute(x, ('fsdp', 'rep'), [(REPLICAS * i + r, REPLICAS * i + t) fo...]
    ppermute x0 -> x3, starting transfers between devices: none -> 3.86 us  [around(): lax.ppermute(x, ('fsdp', 'rep'), [(REPLICAS * i + r, REPLICAS * i + t) fo...]
    all_to_all x3, waiting for transfers between devices: 5.9 us -> 8.7 us  [exchange(): return lax.all_to_all(x, 'fsdp', 0, 0, axis_index_groups=groups, tiled=True)]
    ppermute x8 -> x5, starting transfers between devices: 6.91 us -> 4.14 us  [along_x(): lax.ppermute(x, 'rep', [(i, (i + distance) % REPLICAS) for i in range(REP...]
    ppermute x3, starting transfers between devices: 4.89 us -> 6.58 us  [along_y(): return lax.ppermute(x, 'fsdp', route)]
    all_to_all x3, starting transfers between devices: 18.7 us -> 17 us  [exchange(): return lax.all_to_all(x, 'fsdp', 0, 0, axis_index_groups=groups, tiled=True)]
    pallas_call x2 -> x3, Pallas kernels: 4.07 us -> 2.5 us  [the longest x1 2.5 us: pack_roots(): pl.pallas_call(kernel, name='pack_roots', in_specs=[HBM] * len(roots), ou...]
  transfers between devices with their start and end apart: 15 -> 15, of which waited for: 7 -> 8; matrix products, arithmetic and copies ran while one was open for 0% -> 0% of each run, Pallas kernels for 25% -> 25%
where the time goes in v2:
time: 81.3 us; the launch traced here: 80.9 us
  starting transfers between devices  31.9 us (39%)
  Pallas kernels  25.9 us (32%)
  waiting for transfers between devices  21.5 us (26%)
  between operations  0.9 us (1%)
    all_to_all x3, starting transfers between devices, exchange(): return lax.all_to_all(x, 'fsdp', 0, 0, axis_index_groups=groups, tiled=True)  17 us
    all_to_all x3, waiting for transfers between devices, exchange(): return lax.all_to_all(x, 'fsdp', 0, 0, axis_index_groups=groups, tiled=True)  8.7 us
    ppermute x5, waiting for transfers between devices, along_x(): lax.ppermute(x, 'rep', [(i, (i + distance) % REPLICAS) for i in range(REP...  6.71 us
    ppermute x3, starting transfers between devices, along_y(): return lax.ppermute(x, 'fsdp', route)  6.58 us
    ppermute x3, waiting for transfers between devices, around(): lax.ppermute(x, ('fsdp', 'rep'), [(REPLICAS * i + r, REPLICAS * i + t) fo...  4.8 us
    pallas_call x1, Pallas kernels, apply_whole(): pl.pallas_call(kernel, name='apply_whole', in_specs=[HBM] * (7 + len(root...  4.67 us
    pallas_call x1, Pallas kernels, grams(): pl.pallas_call(kernel, name='grams', in_specs=[HBM] * 7, out_specs=[HBM]...  4.58 us
    pallas_call x1, Pallas kernels, apply_band(): pl.pallas_call(kernel, name='apply_band', in_specs=[HBM] * 6, out_specs=H...  4.54 us
  transfers between devices with their start and end apart: 15, of which 8 were waited for; matrix products, arithmetic and copies ran while one was open for 0% of the time, Pallas kernels for 25%

profile of v2, /device:TPU:1, one launch (start us, length us, event | category | flops | bytes accessed | tf_op | source)
XLA Modules:
  0.0 80.9 jit_solution(3743660903801799915)
XLA Ops:
  0.6 2.4 %deal.1 = f32[8,64,1024]{2,1,0:T(8,128)} custom-call(f32[64,12288]{1,0:T(8,128)} %grad.5), custom_call_target="tpu_custom_call" | custom-call | flops 1 | bytes 1 | tf_op jit(solution)/shard_map/deal/pallas_call | solution.py:105
  3.0 7.5 %all-to-all-start = ((f32[8,64,1024]{2,1,0:T(8,128)}), f32[8,64,1024]{2,1,0:T(8,128)}, u32[]{:S(2)}, u32[]{:S(2)}) async-start(f32[8,64,1024]{2,1,0:T(8,128)} %deal.1), calls=%async_computation | async-start | bytes 4194304 | tf_op jit(solution)/shard_map/all_to_all | solution.py:431
  10.5 1.8 %deal_core.1 = f32[4,64,512]{2,1,0:T(8,128)} custom-call(f32[64,12288]{1,0:T(8,128)} %grad.5), custom_call_target="tpu_custom_call" | custom-call | flops 1 | bytes 1 | tf_op jit(solution)/shard_map/deal_core/pallas_call | solution.py:126
  12.6 2.5 %pack_roots.1 = (f32[4,128,128]{2,1,0:T(8,128)}, f32[5,128,128]{2,1,0:T(8,128)}, f32[5,128,128]{2,1,0:T(8,128)}, f32[5,128,128]{2,1,0:T(8,128)}, f32[5,128,128]{2,1,0:T(8,128)}) custom-call(f32[3,128,512]{2,1,0:T(8,128)} %refs_4_.1, f32[3,128,512]{2,1,0:T(8,128)} %refs_5_.1), custom_call_target="tpu_custom_call" | custom-call | flops 1 | bytes 1 | tf_op jit(solution)/shard_map/pack_roots/pallas_call | solution.py:182
  15.1 1.2 %collective-permute-start.2 = (f32[4,128,128]{2,1,0:T(8,128)}, f32[4,128,128]{2,1,0:T(8,128)S(1)}, u32[]{:S(2)}, u32[]{:S(2)}) collective-permute-start(f32[4,128,128]{2,1,0:T(8,128)} %get-tuple-element.24), channel_id=1, source_target_pairs={{0,2},{1,3},{2,0},{3,1},{4,6},{5,7},{6,4},{7,5},{8,10},{9,11},{10,... | collective-permute-start | bytes 786440 | tf_op jit(solution)/shard_map/ppermute | solution.py:438
  17.8 6.7 %collective-permute-done.2.refs_5_.refs_1_.refs_8_ = f32[4,128,128]{2,1,0:T(8,128)S(1)} collective-permute-done((f32[4,128,128]{2,1,0:T(8,128)}, f32[4,128,128]{2,1,0:T(8,128)S(1)}, u32[]{:S(2)}, u32[]{:S(2)}) %collective-permute-start.2) | collective-permute-done | bytes 262176 | tf_op jit(solution)/shard_map/ppermute | solution.py:438
  26.6 2.1 %pack.1 = (f32[2,64,512]{2,1,0:T(8,128)}, f32[2,64,512]{2,1,0:T(8,128)}, f32[2,64,512]{2,1,0:T(8,128)}, f32[2,64,512]{2,1,0:T(8,128)}) custom-call(f32[64,12288]{1,0:T(8,128)} %grad.5, f32[4,64,512]{2,1,0:T(8,128)} %collective-permute-done.3.got), custom_call_target="tpu_custom_call" | custom-call | flops 1 | bytes 1 | tf_op jit(solution)/shard_map/pack/pallas_call | solution.py:150
  28.8 1.9 %collective-permute-start.4 = (f32[2,64,512]{2,1,0:T(8,128)}, f32[2,64,512]{2,1,0:T(8,128)S(1)}, u32[]{:S(2)}, u32[]{:S(2)}) collective-permute-start(f32[2,64,512]{2,1,0:T(8,128)} %get-tuple-element.26), channel_id=1, source_target_pairs={{0,8},{4,12},{8,16},{12,20},{16,24},{20,28},{24,0},{28,4},{32,40},... | collective-permute-start | bytes 786440 | tf_op jit(solution)/shard_map/ppermute | solution.py:435
  30.7 2.5 %collective-permute-start.5 = (f32[2,64,512]{2,1,0:T(8,128)}, f32[2,64,512]{2,1,0:T(8,128)}, u32[]{:S(2)}, u32[]{:S(2)}) collective-permute-start(f32[2,64,512]{2,1,0:T(8,128)} %get-tuple-element.27), channel_id=1, source_target_pairs={{0,24},{4,28},{8,0},{12,4},{16,8},{20,12},{24,16},{28,20},{32,56},... | collective-permute-start | bytes 786440 | tf_op jit(solution)/shard_map/ppermute | solution.py:435
  33.2 2.1 %collective-permute-start.6 = (f32[2,64,512]{2,1,0:T(8,128)}, f32[2,64,512]{2,1,0:T(8,128)}, u32[]{:S(2)}, u32[]{:S(2)}) collective-permute-start(f32[2,64,512]{2,1,0:T(8,128)} %get-tuple-element.28), channel_id=1, source_target_pairs={{0,16},{4,20},{8,24},{12,28},{16,0},{20,4},{24,8},{28,12},{32,48},... | collective-permute-start | bytes 786440 | tf_op jit(solution)/shard_map/ppermute | solution.py:435
  35.4 1.7 %all-to-all-done = f32[8,64,1024]{2,1,0:T(8,128)} async-done(((f32[8,64,1024]{2,1,0:T(8,128)}), f32[8,64,1024]{2,1,0:T(8,128)}, u32[]{:S(2)}, u32[]{:S(2)}) %all-to-all-start) | async-done | bytes 2097184 | tf_op jit(solution)/shard_map/all_to_all | solution.py:431
  37.0 4.5 %apply_band.1 = f32[512,256]{1,0:T(8,128)} custom-call(f32[512,1024]{1,0:T(8,128)} %bitcast.refs_0_.blocks, f32[3,128,512]{2,1,0:T(8,128)} %refs_4_.1, f32[3,128,512]{2,1,0:T(8,128)} %refs_5_.1, f32[5,128,128]{2,1,0:T(8,128)} %collective-permute-done.refs_3_, f32[5,128,128]{2,1,0:T(8,128)} %collective-permute-done.1.refs_4_, f32[4,128,128]{2,1,0:T(8,128)} %copy-done), custom_call_target="tpu_custom_call" | custom-call | flops 1 | bytes 1 | tf_op jit(solution)/shard_map/apply_band/pallas_call | solution.py:272
  41.6 5.4 %all-to-all-start.1 = ((f32[8,64,256]{2,1,0:T(8,128)}), f32[8,64,256]{2,1,0:T(8,128)}, u32[]{:S(2)}, u32[]{:S(2)}) async-start(f32[8,64,256]{2,1,0:T(8,128)} %bitcast.3), calls=%async_computation.1 | async-start | bytes 1048576 | tf_op jit(solution)/shard_map/all_to_all | solution.py:431
  47.0 1.3 %collective-permute-done.6.refs_3_ = f32[2,64,512]{2,1,0:T(8,128)} collective-permute-done((f32[2,64,512]{2,1,0:T(8,128)}, f32[2,64,512]{2,1,0:T(8,128)}, u32[]{:S(2)}, u32[]{:S(2)}) %collective-permute-start.6) | collective-permute-done | bytes 262176 | tf_op jit(solution)/shard_map/ppermute | solution.py:435
  48.2 4.7 %apply_whole.1 = f32[512,512]{1,0:T(8,128)} custom-call(f32[2,64,512]{2,1,0:T(8,128)} %get-tuple-element.25.refs_0_, f32[2,64,512]{2,1,0:T(8,128)} %copy-done.1, f32[2,64,512]{2,1,0:T(8,128)} %collective-permute-done.5.refs_2_, f32[2,64,512]{2,1,0:T(8,128)} %collective-permute-done.6.refs_3_, f32[3,128,512]{2,1,0:T(8,128)} %refs_4_.1, ...), custom_call_target="tpu_custom_call" | custom-call | flops 137438953472 | bytes 4194304 | tf_op jit(solution)/shard_map/apply_whole/pallas_call | solution.py:320
  52.9 3.6 %all-to-all-done.1.refs_0_ = f32[8,64,256]{2,1,0:T(8,128)} async-done(((f32[8,64,256]{2,1,0:T(8,128)}), f32[8,64,256]{2,1,0:T(8,128)}, u32[]{:S(2)}, u32[]{:S(2)}) %all-to-all-start.1) | async-done | bytes 524320 | tf_op jit(solution)/shard_map/all_to_all | solution.py:431
  57.5 4.2 %all-to-all-start.2 = ((f32[8,64,512]{2,1,0:T(8,128)}), f32[8,64,512]{2,1,0:T(8,128)}, u32[]{:S(2)}, u32[]{:S(2)}) async-start(f32[8,64,512]{2,1,0:T(8,128)} %bitcast.4), calls=%async_computation.2 | async-start | bytes 2097152 | tf_op jit(solution)/shard_map/all_to_all | solution.py:431
  61.7 1.0 %collective-permute-start.10 = (f32[8,64,256]{2,1,0:T(8,128)}, f32[8,64,256]{2,1,0:T(8,128)}, u32[]{:S(2)}, u32[]{:S(2)}) collective-permute-start(f32[8,64,256]{2,1,0:T(8,128)} %all-to-all-done.1.refs_0_), channel_id=1, source_target_pairs={{0,3},{1,0},{2,1},{3,2},{4,5},{5,6},{6,7},{7,4},{8,11},{9,8},{10,9... | collective-permute-start | bytes 1572872 | tf_op jit(solution)/shard_map/ppermute | solution.py:442
  62.7 2.5 %collective-permute-done.9.refs_1_ = f32[8,64,256]{2,1,0:T(8,128)} collective-permute-done((f32[8,64,256]{2,1,0:T(8,128)}, f32[8,64,256]{2,1,0:T(8,128)}, u32[]{:S(2)}, u32[]{:S(2)}) %collective-permute-start.9) | collective-permute-done | bytes 524320 | tf_op jit(solution)/shard_map/ppermute | solution.py:442
  65.2 1.9 %collective-permute-start.11 = (f32[8,64,256]{2,1,0:T(8,128)}, f32[8,64,256]{2,1,0:T(8,128)}, u32[]{:S(2)}, u32[]{:S(2)}) collective-permute-start(f32[8,64,256]{2,1,0:T(8,128)} %collective-permute-done.9.refs_1_), channel_id=1, source_target_pairs={{0,1},{1,2},{2,3},{3,0},{4,7},{5,4},{6,5},{7,6},{8,9},{9,10},{10,1... | collective-permute-start | bytes 1572872 | tf_op jit(solution)/shard_map/ppermute | solution.py:442
  67.1 4.6 %grams.1 = (f32[3,128,512]{2,1,0:T(8,128)}, f32[3,128,512]{2,1,0:T(8,128)}) custom-call(f32[512,1024]{1,0:T(8,128)} %bitcast.refs_0_.blocks, f32[2,64,512]{2,1,0:T(8,128)} %get-tuple-element.25.refs_0_, f32[2,64,512]{2,1,0:T(8,128)} %copy-done.1, f32[2,64,512]{2,1,0:T(8,128)} %collective-permute-done.5.refs_2_, ...), custom_call_target="tpu_custom_call" | custom-call | flops 1 | bytes 1 | tf_op jit(solution)/shard_map/grams/pallas_call | solution.py:364
  71.7 1.7 %collective-permute-done.10.refs_2_ = f32[8,64,256]{2,1,0:T(8,128)} collective-permute-done((f32[8,64,256]{2,1,0:T(8,128)}, f32[8,64,256]{2,1,0:T(8,128)}, u32[]{:S(2)}, u32[]{:S(2)}) %collective-permute-start.10) | collective-permute-done | bytes 524320 | tf_op jit(solution)/shard_map/ppermute | solution.py:442
  73.4 3.4 %all-to-all-done.2.refs_4_ = f32[8,64,512]{2,1,0:T(8,128)} async-done(((f32[8,64,512]{2,1,0:T(8,128)}), f32[8,64,512]{2,1,0:T(8,128)}, u32[]{:S(2)}, u32[]{:S(2)}) %all-to-all-start.2) | async-done | bytes 1048608 | tf_op jit(solution)/shard_map/all_to_all | solution.py:431
  77.4 3.3 %join.1 = f32[64,12288]{1,0:T(8,128)} custom-call(f32[8,64,256]{2,1,0:T(8,128)} %all-to-all-done.1.refs_0_, f32[8,64,256]{2,1,0:T(8,128)} %collective-permute-done.9.refs_1_, f32[8,64,256]{2,1,0:T(8,128)} %collective-permute-done.10.refs_2_, f32[8,64,256]{2,1,0:T(8,128)} %collective-permute-done.11.refs_3_, f32[8,64,512]{2,1,0:T(8,128)} %all-to-all-done.2.refs_4_), custom_call_target="tpu_custom_call" | custom-call | flops 1 | bytes 1 | tf_op jit(solution)/shard_map/join/pallas_call | solution.py:409
  (20 shorter events, 5.5 us)
Async XLA Ops:
  3.0 34.0 %all-to-all-start = ((f32[8,64,1024]{2,1,0:T(8,128)}), f32[8,64,1024]{2,1,0:T(8,128)}, u32[]{:S(2)}, u32[]{:S(2)}) async-start(f32[8,64,1024]{2,1,0:T(8,128)} %deal.1), calls=%async_computation | async-start | bytes 4194304 | tf_op jit(solution)/shard_map/all_to_all | solution.py:431
  12.3 14.3 %collective-permute-start.3 = (f32[4,64,512]{2,1,0:T(8,128)}, f32[4,64,512]{2,1,0:T(8,128)}, u32[]{:S(2)}, u32[]{:S(2)}) collective-permute-start(f32[4,64,512]{2,1,0:T(8,128)} %deal_core.1), channel_id=1, source_target_pairs={{0,4},{4,0},{8,12},{12,8},{16,20},{20,16},{24,28},{28,24},{32,36},... | collective-permute-start | bytes 1572872 | tf_op jit(solution)/shard_map/ppermute | solution.py:445
  15.1 9.4 %collective-permute-start.2 = (f32[4,128,128]{2,1,0:T(8,128)}, f32[4,128,128]{2,1,0:T(8,128)S(1)}, u32[]{:S(2)}, u32[]{:S(2)}) collective-permute-start(f32[4,128,128]{2,1,0:T(8,128)} %get-tuple-element.24), channel_id=1, source_target_pairs={{0,2},{1,3},{2,0},{3,1},{4,6},{5,7},{6,4},{7,5},{8,10},{9,11},{10,... | collective-permute-start | bytes 786440 | tf_op jit(solution)/shard_map/ppermute | solution.py:438
  16.3 14.4 %collective-permute-start = (f32[5,128,128]{2,1,0:T(8,128)}, f32[5,128,128]{2,1,0:T(8,128)}, u32[]{:S(2)}, u32[]{:S(2)}) collective-permute-start(f32[5,128,128]{2,1,0:T(8,128)} %get-tuple-element.22), channel_id=1, source_target_pairs={{0,3},{1,0},{2,1},{3,2},{4,7},{5,4},{6,5},{7,6},{8,11},{9,8},{10,9... | collective-permute-start | bytes 983048 | tf_op jit(solution)/shard_map/ppermute | solution.py:438
  17.2 16.1 %collective-permute-start.1 = (f32[5,128,128]{2,1,0:T(8,128)}, f32[5,128,128]{2,1,0:T(8,128)}, u32[]{:S(2)}, u32[]{:S(2)}) collective-permute-start(f32[5,128,128]{2,1,0:T(8,128)} %get-tuple-element.23), channel_id=1, source_target_pairs={{0,1},{1,2},{2,3},{3,0},{4,5},{5,6},{6,7},{7,4},{8,9},{9,10},{10,1... | collective-permute-start | bytes 983048 | tf_op jit(solution)/shard_map/ppermute | solution.py:438
  24.5 0.7 copy-start
  25.2 21.8 %collective-permute-start.7 = (f32[5,128,128]{2,1,0:T(8,128)}, f32[5,128,128]{2,1,0:T(8,128)}, u32[]{:S(2)}, u32[]{:S(2)}) collective-permute-start(f32[5,128,128]{2,1,0:T(8,128)} %follow.2), channel_id=1, source_target_pairs={{0,3},{1,0},{2,1},{3,2},{4,7},{5,4},{6,5},{7,6},{8,11},{9,8},{10,9... | collective-permute-start | bytes 983048 | tf_op jit(solution)/shard_map/ppermute | solution.py:438
  25.9 21.1 %collective-permute-start.8 = (f32[5,128,128]{2,1,0:T(8,128)}, f32[5,128,128]{2,1,0:T(8,128)}, u32[]{:S(2)}, u32[]{:S(2)}) collective-permute-start(f32[5,128,128]{2,1,0:T(8,128)} %follow.3), channel_id=1, source_target_pairs={{0,1},{1,2},{2,3},{3,0},{4,5},{5,6},{6,7},{7,4},{8,9},{9,10},{10,1... | collective-permute-start | bytes 983048 | tf_op jit(solution)/shard_map/ppermute | solution.py:438
  28.8 18.2 %collective-permute-start.4 = (f32[2,64,512]{2,1,0:T(8,128)}, f32[2,64,512]{2,1,0:T(8,128)S(1)}, u32[]{:S(2)}, u32[]{:S(2)}) collective-permute-start(f32[2,64,512]{2,1,0:T(8,128)} %get-tuple-element.26), channel_id=1, source_target_pairs={{0,8},{4,12},{8,16},{12,20},{16,24},{20,28},{24,0},{28,4},{32,40},... | collective-permute-start | bytes 786440 | tf_op jit(solution)/shard_map/ppermute | solution.py:435
  30.7 16.3 %collective-permute-start.5 = (f32[2,64,512]{2,1,0:T(8,128)}, f32[2,64,512]{2,1,0:T(8,128)}, u32[]{:S(2)}, u32[]{:S(2)}) collective-permute-start(f32[2,64,512]{2,1,0:T(8,128)} %get-tuple-element.27), channel_id=1, source_target_pairs={{0,24},{4,28},{8,0},{12,4},{16,8},{20,12},{24,16},{28,20},{32,56},... | collective-permute-start | bytes 786440 | tf_op jit(solution)/shard_map/ppermute | solution.py:435
  33.2 15.0 %collective-permute-start.6 = (f32[2,64,512]{2,1,0:T(8,128)}, f32[2,64,512]{2,1,0:T(8,128)}, u32[]{:S(2)}, u32[]{:S(2)}) collective-permute-start(f32[2,64,512]{2,1,0:T(8,128)} %get-tuple-element.28), channel_id=1, source_target_pairs={{0,16},{4,20},{8,24},{12,28},{16,0},{20,4},{24,8},{28,12},{32,48},... | collective-permute-start | bytes 786440 | tf_op jit(solution)/shard_map/ppermute | solution.py:435
  41.6 15.0 %all-to-all-start.1 = ((f32[8,64,256]{2,1,0:T(8,128)}), f32[8,64,256]{2,1,0:T(8,128)}, u32[]{:S(2)}, u32[]{:S(2)}) async-start(f32[8,64,256]{2,1,0:T(8,128)} %bitcast.3), calls=%async_computation.1 | async-start | bytes 1048576 | tf_op jit(solution)/shard_map/all_to_all | solution.py:431
  47.0 1.3 %copy-start.1 = (f32[2,64,512]{2,1,0:T(8,128)}, f32[2,64,512]{2,1,0:T(8,128)S(1)}, u32[]{:S(2)}) copy-start(f32[2,64,512]{2,1,0:T(8,128)S(1)} %collective-permute-done.4.refs_1_) | copy-start | bytes 786436
  56.5 8.6 %collective-permute-start.9 = (f32[8,64,256]{2,1,0:T(8,128)}, f32[8,64,256]{2,1,0:T(8,128)}, u32[]{:S(2)}, u32[]{:S(2)}) collective-permute-start(f32[8,64,256]{2,1,0:T(8,128)} %all-to-all-done.1.refs_0_), channel_id=1, source_target_pairs={{0,1},{1,2},{2,3},{3,0},{4,7},{5,4},{6,5},{7,6},{8,9},{9,10},{10,1... | collective-permute-start | bytes 1572872 | tf_op jit(solution)/shard_map/ppermute | solution.py:442
  57.5 19.3 %all-to-all-start.2 = ((f32[8,64,512]{2,1,0:T(8,128)}), f32[8,64,512]{2,1,0:T(8,128)}, u32[]{:S(2)}, u32[]{:S(2)}) async-start(f32[8,64,512]{2,1,0:T(8,128)} %bitcast.4), calls=%async_computation.2 | async-start | bytes 2097152 | tf_op jit(solution)/shard_map/all_to_all | solution.py:431
  61.7 11.6 %collective-permute-start.10 = (f32[8,64,256]{2,1,0:T(8,128)}, f32[8,64,256]{2,1,0:T(8,128)}, u32[]{:S(2)}, u32[]{:S(2)}) collective-permute-start(f32[8,64,256]{2,1,0:T(8,128)} %all-to-all-done.1.refs_0_), channel_id=1, source_target_pairs={{0,3},{1,0},{2,1},{3,2},{4,5},{5,6},{6,7},{7,4},{8,11},{9,8},{10,9... | collective-permute-start | bytes 1572872 | tf_op jit(solution)/shard_map/ppermute | solution.py:442
  65.2 12.2 %collective-permute-start.11 = (f32[8,64,256]{2,1,0:T(8,128)}, f32[8,64,256]{2,1,0:T(8,128)}, u32[]{:S(2)}, u32[]{:S(2)}) collective-permute-start(f32[8,64,256]{2,1,0:T(8,128)} %collective-permute-done.9.refs_1_), channel_id=1, source_target_pairs={{0,1},{1,2},{2,3},{3,0},{4,7},{5,4},{6,5},{7,6},{8,9},{9,10},{10,1... | collective-permute-start | bytes 1572872 | tf_op jit(solution)/shard_map/ppermute | solution.py:442

commit v3 on v2

--- a/solution.py
+++ b/solution.py
@@ -49,6 +49,12 @@
 
     both = one(a, b[0])
     return both[:rows] + (both[rows:] + one(a[:rows], b[1]))
+
+
+def dot_beside(a, b):
+    columns = b.shape[1] // 2
+    both = jnp.dot(a[0], b, preferred_element_type=F32)
+    return both[:, :columns] + (both[:, columns:] + jnp.dot(a[1], b[:, :columns], preferred_element_type=F32))
 
 
 def dot3(a, b, dims):
@@ -261,9 +267,9 @@
             assemble(i, bands, above, below, across, whole)
             left_root = split(whole[...])
             loads[i].wait()
-            half = dot_stacked(stacked(right_v[i]), split(grad[i]), ((1,), (1,)))
+            half = dot_beside(split(grad[i]), stacked(right_v[i]).T)
             columns = pl.ds(i * BAND, BAND)
-            result[:, columns] = dot_stacked(stacked(half), left_root, ((1,), (0,))).T
+            result[:, columns] = dot_beside(left_root, jnp.concatenate(split(half), axis=1))
             stores.append(pltpu.make_async_copy(result.at[:, columns], out.at[:, columns], sems.at[i]))
             stores[-1].start()
         for copy in stores:

time: 81.3 us -> 81.1 us (level)
  no operation moved by 1% of the time
where the time goes in v3:
time: 81.1 us; the launch traced here: 80.7 us
  starting transfers between devices  31.9 us (39%)
  Pallas kernels  25.7 us (32%)
  waiting for transfers between devices  21.5 us (27%)
  between operations  0.9 us (1%)
    all_to_all x3, starting transfers between devices, exchange(): return lax.all_to_all(x, 'fsdp', 0, 0, axis_index_groups=groups, tiled=True)  17 us
    all_to_all x3, waiting for transfers between devices, exchange(): return lax.all_to_all(x, 'fsdp', 0, 0, axis_index_groups=groups, tiled=True)  8.51 us
    ppermute x5, waiting for transfers between devices, along_x(): lax.ppermute(x, 'rep', [(i, (i + distance) % REPLICAS) for i in range(REP...  6.71 us
    ppermute x3, starting transfers between devices, along_y(): return lax.ppermute(x, 'fsdp', route)  6.58 us
    ppermute x3, waiting for transfers between devices, around(): lax.ppermute(x, ('fsdp', 'rep'), [(REPLICAS * i + r, REPLICAS * i + t) fo...  4.82 us
    pallas_call x1, Pallas kernels, apply_whole(): pl.pallas_call(kernel, name='apply_whole', in_specs=[HBM] * (7 + len(root...  4.67 us
    pallas_call x1, Pallas kernels, grams(): pl.pallas_call(kernel, name='grams', in_specs=[HBM] * 7, out_specs=[HBM]...  4.56 us
    pallas_call x1, Pallas kernels, apply_band(): pl.pallas_call(kernel, name='apply_band', in_specs=[HBM] * 6, out_specs=H...  4.36 us
  transfers between devices with their start and end apart: 15, of which 8 were waited for; matrix products, arithmetic and copies ran while one was open for 0% of the time, Pallas kernels for 25%

profile of v3, /device:TPU:1, one launch (start us, length us, event | category | flops | bytes accessed | tf_op | source)
XLA Modules:
  0.0 80.7 jit_solution(9117231825372826369)
XLA Ops:
  0.6 2.4 %deal.1 = f32[8,64,1024]{2,1,0:T(8,128)} custom-call(f32[64,12288]{1,0:T(8,128)} %grad.5), custom_call_target="tpu_custom_call" | custom-call | flops 1 | bytes 1 | tf_op jit(solution)/shard_map/deal/pallas_call | solution.py:111
  3.0 7.5 %all-to-all-start = ((f32[8,64,1024]{2,1,0:T(8,128)}), f32[8,64,1024]{2,1,0:T(8,128)}, u32[]{:S(2)}, u32[]{:S(2)}) async-start(f32[8,64,1024]{2,1,0:T(8,128)} %deal.1), calls=%async_computation | async-start | bytes 4194304 | tf_op jit(solution)/shard_map/all_to_all | solution.py:437
  10.5 1.8 %deal_core.1 = f32[4,64,512]{2,1,0:T(8,128)} custom-call(f32[64,12288]{1,0:T(8,128)} %grad.5), custom_call_target="tpu_custom_call" | custom-call | flops 1 | bytes 1 | tf_op jit(solution)/shard_map/deal_core/pallas_call | solution.py:132
  12.6 2.5 %pack_roots.1 = (f32[4,128,128]{2,1,0:T(8,128)}, f32[5,128,128]{2,1,0:T(8,128)}, f32[5,128,128]{2,1,0:T(8,128)}, f32[5,128,128]{2,1,0:T(8,128)}, f32[5,128,128]{2,1,0:T(8,128)}) custom-call(f32[3,128,512]{2,1,0:T(8,128)} %refs_4_.1, f32[3,128,512]{2,1,0:T(8,128)} %refs_5_.1), custom_call_target="tpu_custom_call" | custom-call | flops 1 | bytes 1 | tf_op jit(solution)/shard_map/pack_roots/pallas_call | solution.py:188
  15.1 1.2 %collective-permute-start.2 = (f32[4,128,128]{2,1,0:T(8,128)}, f32[4,128,128]{2,1,0:T(8,128)S(1)}, u32[]{:S(2)}, u32[]{:S(2)}) collective-permute-start(f32[4,128,128]{2,1,0:T(8,128)} %get-tuple-element.24), channel_id=1, source_target_pairs={{0,2},{1,3},{2,0},{3,1},{4,6},{5,7},{6,4},{7,5},{8,10},{9,11},{10,... | collective-permute-start | bytes 786440 | tf_op jit(solution)/shard_map/ppermute | solution.py:444
  17.8 6.7 %collective-permute-done.2.refs_5_.refs_1_.refs_8_ = f32[4,128,128]{2,1,0:T(8,128)S(1)} collective-permute-done((f32[4,128,128]{2,1,0:T(8,128)}, f32[4,128,128]{2,1,0:T(8,128)S(1)}, u32[]{:S(2)}, u32[]{:S(2)}) %collective-permute-start.2) | collective-permute-done | bytes 262176 | tf_op jit(solution)/shard_map/ppermute | solution.py:444
  26.6 2.1 %pack.1 = (f32[2,64,512]{2,1,0:T(8,128)}, f32[2,64,512]{2,1,0:T(8,128)}, f32[2,64,512]{2,1,0:T(8,128)}, f32[2,64,512]{2,1,0:T(8,128)}) custom-call(f32[64,12288]{1,0:T(8,128)} %grad.5, f32[4,64,512]{2,1,0:T(8,128)} %collective-permute-done.3.got), custom_call_target="tpu_custom_call" | custom-call | flops 1 | bytes 1 | tf_op jit(solution)/shard_map/pack/pallas_call | solution.py:156
  28.8 1.9 %collective-permute-start.4 = (f32[2,64,512]{2,1,0:T(8,128)}, f32[2,64,512]{2,1,0:T(8,128)S(1)}, u32[]{:S(2)}, u32[]{:S(2)}) collective-permute-start(f32[2,64,512]{2,1,0:T(8,128)} %get-tuple-element.26), channel_id=1, source_target_pairs={{0,8},{4,12},{8,16},{12,20},{16,24},{20,28},{24,0},{28,4},{32,40},... | collective-permute-start | bytes 786440 | tf_op jit(solution)/shard_map/ppermute | solution.py:441
  30.7 2.5 %collective-permute-start.5 = (f32[2,64,512]{2,1,0:T(8,128)}, f32[2,64,512]{2,1,0:T(8,128)}, u32[]{:S(2)}, u32[]{:S(2)}) collective-permute-start(f32[2,64,512]{2,1,0:T(8,128)} %get-tuple-element.27), channel_id=1, source_target_pairs={{0,24},{4,28},{8,0},{12,4},{16,8},{20,12},{24,16},{28,20},{32,56},... | collective-permute-start | bytes 786440 | tf_op jit(solution)/shard_map/ppermute | solution.py:441
  33.2 2.1 %collective-permute-start.6 = (f32[2,64,512]{2,1,0:T(8,128)}, f32[2,64,512]{2,1,0:T(8,128)}, u32[]{:S(2)}, u32[]{:S(2)}) collective-permute-start(f32[2,64,512]{2,1,0:T(8,128)} %get-tuple-element.28), channel_id=1, source_target_pairs={{0,16},{4,20},{8,24},{12,28},{16,0},{20,4},{24,8},{28,12},{32,48},... | collective-permute-start | bytes 786440 | tf_op jit(solution)/shard_map/ppermute | solution.py:441
  35.4 1.7 %all-to-all-done = f32[8,64,1024]{2,1,0:T(8,128)} async-done(((f32[8,64,1024]{2,1,0:T(8,128)}), f32[8,64,1024]{2,1,0:T(8,128)}, u32[]{:S(2)}, u32[]{:S(2)}) %all-to-all-start) | async-done | bytes 2097184 | tf_op jit(solution)/shard_map/all_to_all | solution.py:437
  37.0 4.4 %apply_band.1 = f32[512,256]{1,0:T(8,128)} custom-call(f32[512,1024]{1,0:T(8,128)} %bitcast.refs_0_.blocks, f32[3,128,512]{2,1,0:T(8,128)} %refs_4_.1, f32[3,128,512]{2,1,0:T(8,128)} %refs_5_.1, f32[5,128,128]{2,1,0:T(8,128)} %collective-permute-done.refs_3_, f32[5,128,128]{2,1,0:T(8,128)} %collective-permute-done.1.refs_4_, f32[4,128,128]{2,1,0:T(8,128)} %copy-done), custom_call_target="tpu_custom_call" | custom-call | flops 1 | bytes 1 | tf_op jit(solution)/shard_map/apply_band/pallas_call | solution.py:278
  41.4 5.4 %all-to-all-start.1 = ((f32[8,64,256]{2,1,0:T(8,128)}), f32[8,64,256]{2,1,0:T(8,128)}, u32[]{:S(2)}, u32[]{:S(2)}) async-start(f32[8,64,256]{2,1,0:T(8,128)} %bitcast.3), calls=%async_computation.1 | async-start | bytes 1048576 | tf_op jit(solution)/shard_map/all_to_all | solution.py:437
  46.8 1.4 %collective-permute-done.6.refs_3_ = f32[2,64,512]{2,1,0:T(8,128)} collective-permute-done((f32[2,64,512]{2,1,0:T(8,128)}, f32[2,64,512]{2,1,0:T(8,128)}, u32[]{:S(2)}, u32[]{:S(2)}) %collective-permute-start.6) | collective-permute-done | bytes 262176 | tf_op jit(solution)/shard_map/ppermute | solution.py:441
  48.2 4.7 %apply_whole.1 = f32[512,512]{1,0:T(8,128)} custom-call(f32[2,64,512]{2,1,0:T(8,128)} %get-tuple-element.25.refs_0_, f32[2,64,512]{2,1,0:T(8,128)} %copy-done.1, f32[2,64,512]{2,1,0:T(8,128)} %collective-permute-done.5.refs_2_, f32[2,64,512]{2,1,0:T(8,128)} %collective-permute-done.6.refs_3_, f32[3,128,512]{2,1,0:T(8,128)} %refs_4_.1, ...), custom_call_target="tpu_custom_call" | custom-call | flops 137438953472 | bytes 4194304 | tf_op jit(solution)/shard_map/apply_whole/pallas_call | solution.py:326
  52.9 3.4 %all-to-all-done.1.refs_0_ = f32[8,64,256]{2,1,0:T(8,128)} async-done(((f32[8,64,256]{2,1,0:T(8,128)}), f32[8,64,256]{2,1,0:T(8,128)}, u32[]{:S(2)}, u32[]{:S(2)}) %all-to-all-start.1) | async-done | bytes 524320 | tf_op jit(solution)/shard_map/all_to_all | solution.py:437
  57.3 4.2 %all-to-all-start.2 = ((f32[8,64,512]{2,1,0:T(8,128)}), f32[8,64,512]{2,1,0:T(8,128)}, u32[]{:S(2)}, u32[]{:S(2)}) async-start(f32[8,64,512]{2,1,0:T(8,128)} %bitcast.4), calls=%async_computation.2 | async-start | bytes 2097152 | tf_op jit(solution)/shard_map/all_to_all | solution.py:437
  61.5 1.0 %collective-permute-start.10 = (f32[8,64,256]{2,1,0:T(8,128)}, f32[8,64,256]{2,1,0:T(8,128)}, u32[]{:S(2)}, u32[]{:S(2)}) collective-permute-start(f32[8,64,256]{2,1,0:T(8,128)} %all-to-all-done.1.refs_0_), channel_id=1, source_target_pairs={{0,3},{1,0},{2,1},{3,2},{4,5},{5,6},{6,7},{7,4},{8,11},{9,8},{10,9... | collective-permute-start | bytes 1572872 | tf_op jit(solution)/shard_map/ppermute | solution.py:448
  62.5 2.5 %collective-permute-done.9.refs_1_ = f32[8,64,256]{2,1,0:T(8,128)} collective-permute-done((f32[8,64,256]{2,1,0:T(8,128)}, f32[8,64,256]{2,1,0:T(8,128)}, u32[]{:S(2)}, u32[]{:S(2)}) %collective-permute-start.9) | collective-permute-done | bytes 524320 | tf_op jit(solution)/shard_map/ppermute | solution.py:448
  65.0 1.9 %collective-permute-start.11 = (f32[8,64,256]{2,1,0:T(8,128)}, f32[8,64,256]{2,1,0:T(8,128)}, u32[]{:S(2)}, u32[]{:S(2)}) collective-permute-start(f32[8,64,256]{2,1,0:T(8,128)} %collective-permute-done.9.refs_1_), channel_id=1, source_target_pairs={{0,1},{1,2},{2,3},{3,0},{4,7},{5,4},{6,5},{7,6},{8,9},{9,10},{10,1... | collective-permute-start | bytes 1572872 | tf_op jit(solution)/shard_map/ppermute | solution.py:448
  66.9 4.6 %grams.1 = (f32[3,128,512]{2,1,0:T(8,128)}, f32[3,128,512]{2,1,0:T(8,128)}) custom-call(f32[512,1024]{1,0:T(8,128)} %bitcast.refs_0_.blocks, f32[2,64,512]{2,1,0:T(8,128)} %get-tuple-element.25.refs_0_, f32[2,64,512]{2,1,0:T(8,128)} %copy-done.1, f32[2,64,512]{2,1,0:T(8,128)} %collective-permute-done.5.refs_2_, ...), custom_call_target="tpu_custom_call" | custom-call | flops 1 | bytes 1 | tf_op jit(solution)/shard_map/grams/pallas_call | solution.py:370
  71.4 1.7 %collective-permute-done.10.refs_2_ = f32[8,64,256]{2,1,0:T(8,128)} collective-permute-done((f32[8,64,256]{2,1,0:T(8,128)}, f32[8,64,256]{2,1,0:T(8,128)}, u32[]{:S(2)}, u32[]{:S(2)}) %collective-permute-start.10) | collective-permute-done | bytes 524320 | tf_op jit(solution)/shard_map/ppermute | solution.py:448
  73.2 3.4 %all-to-all-done.2.refs_4_ = f32[8,64,512]{2,1,0:T(8,128)} async-done(((f32[8,64,512]{2,1,0:T(8,128)}), f32[8,64,512]{2,1,0:T(8,128)}, u32[]{:S(2)}, u32[]{:S(2)}) %all-to-all-start.2) | async-done | bytes 1048608 | tf_op jit(solution)/shard_map/all_to_all | solution.py:437
  77.2 3.3 %join.1 = f32[64,12288]{1,0:T(8,128)} custom-call(f32[8,64,256]{2,1,0:T(8,128)} %all-to-all-done.1.refs_0_, f32[8,64,256]{2,1,0:T(8,128)} %collective-permute-done.9.refs_1_, f32[8,64,256]{2,1,0:T(8,128)} %collective-permute-done.10.refs_2_, f32[8,64,256]{2,1,0:T(8,128)} %collective-permute-done.11.refs_3_, f32[8,64,512]{2,1,0:T(8,128)} %all-to-all-done.2.refs_4_), custom_call_target="tpu_custom_call" | custom-call | flops 1 | bytes 1 | tf_op jit(solution)/shard_map/join/pallas_call | solution.py:415
  (20 shorter events, 5.5 us)
Async XLA Ops:
  3.0 34.0 %all-to-all-start = ((f32[8,64,1024]{2,1,0:T(8,128)}), f32[8,64,1024]{2,1,0:T(8,128)}, u32[]{:S(2)}, u32[]{:S(2)}) async-start(f32[8,64,1024]{2,1,0:T(8,128)} %deal.1), calls=%async_computation | async-start | bytes 4194304 | tf_op jit(solution)/shard_map/all_to_all | solution.py:437
  12.3 14.3 %collective-permute-start.3 = (f32[4,64,512]{2,1,0:T(8,128)}, f32[4,64,512]{2,1,0:T(8,128)}, u32[]{:S(2)}, u32[]{:S(2)}) collective-permute-start(f32[4,64,512]{2,1,0:T(8,128)} %deal_core.1), channel_id=1, source_target_pairs={{0,4},{4,0},{8,12},{12,8},{16,20},{20,16},{24,28},{28,24},{32,36},... | collective-permute-start | bytes 1572872 | tf_op jit(solution)/shard_map/ppermute | solution.py:451
  15.1 9.4 %collective-permute-start.2 = (f32[4,128,128]{2,1,0:T(8,128)}, f32[4,128,128]{2,1,0:T(8,128)S(1)}, u32[]{:S(2)}, u32[]{:S(2)}) collective-permute-start(f32[4,128,128]{2,1,0:T(8,128)} %get-tuple-element.24), channel_id=1, source_target_pairs={{0,2},{1,3},{2,0},{3,1},{4,6},{5,7},{6,4},{7,5},{8,10},{9,11},{10,... | collective-permute-start | bytes 786440 | tf_op jit(solution)/shard_map/ppermute | solution.py:444
  16.3 14.4 %collective-permute-start = (f32[5,128,128]{2,1,0:T(8,128)}, f32[5,128,128]{2,1,0:T(8,128)}, u32[]{:S(2)}, u32[]{:S(2)}) collective-permute-start(f32[5,128,128]{2,1,0:T(8,128)} %get-tuple-element.22), channel_id=1, source_target_pairs={{0,3},{1,0},{2,1},{3,2},{4,7},{5,4},{6,5},{7,6},{8,11},{9,8},{10,9... | collective-permute-start | bytes 983048 | tf_op jit(solution)/shard_map/ppermute | solution.py:444
  17.2 16.1 %collective-permute-start.1 = (f32[5,128,128]{2,1,0:T(8,128)}, f32[5,128,128]{2,1,0:T(8,128)}, u32[]{:S(2)}, u32[]{:S(2)}) collective-permute-start(f32[5,128,128]{2,1,0:T(8,128)} %get-tuple-element.23), channel_id=1, source_target_pairs={{0,1},{1,2},{2,3},{3,0},{4,5},{5,6},{6,7},{7,4},{8,9},{9,10},{10,1... | collective-permute-start | bytes 983048 | tf_op jit(solution)/shard_map/ppermute | solution.py:444
  24.5 0.7 copy-start
  25.2 21.6 %collective-permute-start.7 = (f32[5,128,128]{2,1,0:T(8,128)}, f32[5,128,128]{2,1,0:T(8,128)}, u32[]{:S(2)}, u32[]{:S(2)}) collective-permute-start(f32[5,128,128]{2,1,0:T(8,128)} %follow.2), channel_id=1, source_target_pairs={{0,3},{1,0},{2,1},{3,2},{4,7},{5,4},{6,5},{7,6},{8,11},{9,8},{10,9... | collective-permute-start | bytes 983048 | tf_op jit(solution)/shard_map/ppermute | solution.py:444
  25.9 20.9 %collective-permute-start.8 = (f32[5,128,128]{2,1,0:T(8,128)}, f32[5,128,128]{2,1,0:T(8,128)}, u32[]{:S(2)}, u32[]{:S(2)}) collective-permute-start(f32[5,128,128]{2,1,0:T(8,128)} %follow.3), channel_id=1, source_target_pairs={{0,1},{1,2},{2,3},{3,0},{4,5},{5,6},{6,7},{7,4},{8,9},{9,10},{10,1... | collective-permute-start | bytes 983048 | tf_op jit(solution)/shard_map/ppermute | solution.py:444
  28.8 18.0 %collective-permute-start.4 = (f32[2,64,512]{2,1,0:T(8,128)}, f32[2,64,512]{2,1,0:T(8,128)S(1)}, u32[]{:S(2)}, u32[]{:S(2)}) collective-permute-start(f32[2,64,512]{2,1,0:T(8,128)} %get-tuple-element.26), channel_id=1, source_target_pairs={{0,8},{4,12},{8,16},{12,20},{16,24},{20,28},{24,0},{28,4},{32,40},... | collective-permute-start | bytes 786440 | tf_op jit(solution)/shard_map/ppermute | solution.py:441
  30.7 16.1 %collective-permute-start.5 = (f32[2,64,512]{2,1,0:T(8,128)}, f32[2,64,512]{2,1,0:T(8,128)}, u32[]{:S(2)}, u32[]{:S(2)}) collective-permute-start(f32[2,64,512]{2,1,0:T(8,128)} %get-tuple-element.27), channel_id=1, source_target_pairs={{0,24},{4,28},{8,0},{12,4},{16,8},{20,12},{24,16},{28,20},{32,56},... | collective-permute-start | bytes 786440 | tf_op jit(solution)/shard_map/ppermute | solution.py:441
  33.2 15.0 %collective-permute-start.6 = (f32[2,64,512]{2,1,0:T(8,128)}, f32[2,64,512]{2,1,0:T(8,128)}, u32[]{:S(2)}, u32[]{:S(2)}) collective-permute-start(f32[2,64,512]{2,1,0:T(8,128)} %get-tuple-element.28), channel_id=1, source_target_pairs={{0,16},{4,20},{8,24},{12,28},{16,0},{20,4},{24,8},{28,12},{32,48},... | collective-permute-start | bytes 786440 | tf_op jit(solution)/shard_map/ppermute | solution.py:441
  41.4 15.0 %all-to-all-start.1 = ((f32[8,64,256]{2,1,0:T(8,128)}), f32[8,64,256]{2,1,0:T(8,128)}, u32[]{:S(2)}, u32[]{:S(2)}) async-start(f32[8,64,256]{2,1,0:T(8,128)} %bitcast.3), calls=%async_computation.1 | async-start | bytes 1048576 | tf_op jit(solution)/shard_map/all_to_all | solution.py:437
  46.8 1.5 %copy-start.1 = (f32[2,64,512]{2,1,0:T(8,128)}, f32[2,64,512]{2,1,0:T(8,128)S(1)}, u32[]{:S(2)}) copy-start(f32[2,64,512]{2,1,0:T(8,128)S(1)} %collective-permute-done.4.refs_1_) | copy-start | bytes 786436
  56.4 8.6 %collective-permute-start.9 = (f32[8,64,256]{2,1,0:T(8,128)}, f32[8,64,256]{2,1,0:T(8,128)}, u32[]{:S(2)}, u32[]{:S(2)}) collective-permute-start(f32[8,64,256]{2,1,0:T(8,128)} %all-to-all-done.1.refs_0_), channel_id=1, source_target_pairs={{0,1},{1,2},{2,3},{3,0},{4,7},{5,4},{6,5},{7,6},{8,9},{9,10},{10,1... | collective-permute-start | bytes 1572872 | tf_op jit(solution)/shard_map/ppermute | solution.py:448
  57.3 19.3 %all-to-all-start.2 = ((f32[8,64,512]{2,1,0:T(8,128)}), f32[8,64,512]{2,1,0:T(8,128)}, u32[]{:S(2)}, u32[]{:S(2)}) async-start(f32[8,64,512]{2,1,0:T(8,128)} %bitcast.4), calls=%async_computation.2 | async-start | bytes 2097152 | tf_op jit(solution)/shard_map/all_to_all | solution.py:437
  61.5 11.6 %collective-permute-start.10 = (f32[8,64,256]{2,1,0:T(8,128)}, f32[8,64,256]{2,1,0:T(8,128)}, u32[]{:S(2)}, u32[]{:S(2)}) collective-permute-start(f32[8,64,256]{2,1,0:T(8,128)} %all-to-all-done.1.refs_0_), channel_id=1, source_target_pairs={{0,3},{1,0},{2,1},{3,2},{4,5},{5,6},{6,7},{7,4},{8,11},{9,8},{10,9... | collective-permute-start | bytes 1572872 | tf_op jit(solution)/shard_map/ppermute | solution.py:448
  65.0 12.2 %collective-permute-start.11 = (f32[8,64,256]{2,1,0:T(8,128)}, f32[8,64,256]{2,1,0:T(8,128)}, u32[]{:S(2)}, u32[]{:S(2)}) collective-permute-start(f32[8,64,256]{2,1,0:T(8,128)} %collective-permute-done.9.refs_1_), channel_id=1, source_target_pairs={{0,1},{1,2},{2,3},{3,0},{4,7},{5,4},{6,5},{7,6},{8,9},{9,10},{10,1... | collective-permute-start | bytes 1572872 | tf_op jit(solution)/shard_map/ppermute | solution.py:448

commit v4 on v3

--- a/solution.py
+++ b/solution.py
@@ -17,7 +17,9 @@
 FILLED = 2
 SHIFTS = (1, 3, 2)
 HBM = pl.BlockSpec(memory_space=pltpu.HBM)
+VMEM = pl.BlockSpec(memory_space=pltpu.VMEM)
 PARAMS = pltpu.CompilerParams(vmem_limit_bytes=63 * 1024 * 1024 + 512 * 1024)
+SMALL = pltpu.CompilerParams(vmem_limit_bytes=32 * 1024 * 1024)
 
 
 def array(*shape, dtype=F32):
@@ -378,7 +380,7 @@
             pltpu.VMEM((2, SLOTS, BAND, BLOCK), F32),
             pltpu.SemaphoreType.DMA((SLOTS, 12)),
         ],
-        compiler_params=PARAMS,
+        compiler_params=SMALL,
         cost_estimate=cost(36 * BLOCK * BLOCK * BAND, 7 << 20),
     )(blocks, *pieces, left_stat, right_stat)
 
@@ -386,45 +388,40 @@
 def join(pieces, filled):
     n = len(BANDED)
 
-    def kernel(*refs):
-        *pieces, filled, out, bands, blocks, rows, sems = refs
+    def kernel(own, near, other, far, filled, out, own_v, rows, sems):
         _, core, me = place()
-        sources = [me, lax.rem(me + 3 - 2 * core, 4), lax.rem(me + 1 + 2 * core, 4), lax.rem(me + 2, 4)]
-        loads = []
-        for owner in range(8):
-            pairs = [(piece.at[owner], bands.at[i, owner]) for i, piece in enumerate(pieces)]
-            pairs.append((filled.at[owner], blocks.at[owner]))
-            loads.append([pltpu.make_async_copy(a, b, sems.at[owner, i]) for i, (a, b) in enumerate(pairs)])
-            for copy in loads[-1]:
-                copy.start()
+        load = pltpu.make_async_copy(own, own_v, sems.at[8, 0])
+        load.start()
         stores = []
         for owner in range(8):
-            for copy in loads[owner]:
-                copy.wait()
+            target = out.at[:, pl.ds((SLOTS * owner + FILLED) * BLOCK, BLOCK)]
+            stores.append(pltpu.make_async_copy(filled.at[owner], target, sems.at[owner, 0]))
+            stores[-1].start()
+        sources = (lax.rem(me + 3 - 2 * core, 4), lax.rem(me + 1 + 2 * core, 4), lax.rem(me + 2, 4), me)
+        load.wait()
+        for owner in range(8):
             for j, slot in enumerate(BANDED):
-                for i, source in enumerate(sources):
-                    rows[owner, :, at(j * REPLICAS + source)] = bands[i, owner, :, j * BAND : (j + 1) * BAND]
-            targets = [(rows.at[owner, :, pl.ds(j * BLOCK, BLOCK)], slot) for j, slot in enumerate(BANDED)]
-            for j, (source, slot) in enumerate(targets + [(blocks.at[owner], FILLED)]):
+                for bands, source in zip((near, other, far, own_v), sources):
+                    rows[owner, :, at(j * REPLICAS + source)] = bands[owner, :, j * BAND : (j + 1) * BAND]
                 target = out.at[:, pl.ds((SLOTS * owner + slot) * BLOCK, BLOCK)]
-                stores.append(pltpu.make_async_copy(source, target, sems.at[owner, REPLICAS + 1 + j]))
-                stores[-1].start()
+                copy = pltpu.make_async_copy(rows.at[owner, :, pl.ds(j * BLOCK, BLOCK)], target, sems.at[owner, 1 + j])
+                copy.start()
+                stores.append(copy)
         for copy in stores:
             copy.wait()
 
     return pl.pallas_call(
         kernel,
         name="join",
-        in_specs=[HBM] * (REPLICAS + 1),
+        in_specs=[HBM] + [VMEM] * 4,
         out_specs=HBM,
         out_shape=array(64, 8 * OWNED),
         scratch_shapes=[
-            pltpu.VMEM((REPLICAS, 8, 64, n * BAND), F32),
-            pltpu.VMEM((8, 64, BLOCK), F32),
+            pltpu.VMEM((8, 64, n * BAND), F32),
             pltpu.VMEM((8, 64, n * BLOCK), F32),
-            pltpu.SemaphoreType.DMA((8, REPLICAS + 1 + SLOTS)),
+            pltpu.SemaphoreType.DMA((9, 1 + n)),
         ],
-        compiler_params=PARAMS,
+        compiler_params=SMALL,
         cost_estimate=cost(0, 6 << 20),
     )(*pieces, filled)
 

time: 81.1 us -> 80.9 us (level); the launches traced: 80.7 us -> 79.6 us
  local copies, waits for them, and re-layouts: 0.71 us -> 3.92 us
  waiting for transfers between devices: 21.5 us -> 18.7 us
  starting transfers between devices: 31.9 us -> 30.8 us
    unnamed x4 -> x12, local copies, waits for them, and re-layouts: 0.71 us -> 3.92 us
    all_to_all x3, waiting for transfers between devices: 8.51 us -> 6.47 us  [exchange(): return lax.all_to_all(x, 'fsdp', 0, 0, axis_index_groups=groups, tiled=True)]
  transfers between devices with their start and end apart: 15 -> 15, of which waited for: 8 -> 7; matrix products, arithmetic and copies ran while one was open for 0% -> 0% of each run, Pallas kernels for 25% -> 25%
where the time goes in v4:
time: 80.9 us; the launch traced here: 79.6 us
  starting transfers between devices  30.8 us (38%)
  Pallas kernels  25.3 us (31%)
  waiting for transfers between devices  18.7 us (23%)
  local copies, waits for them, and re-layouts  3.92 us (5%)
  between operations  0.91 us (1%)
    all_to_all x3, starting transfers between devices, exchange(): return lax.all_to_all(x, 'fsdp', 0, 0, axis_index_groups=groups, tiled=True)  16.4 us
    ppermute x5, waiting for transfers between devices, along_x(): lax.ppermute(x, 'rep', [(i, (i + distance) % REPLICAS) for i in range(REP...  6.71 us
    ppermute x3, starting transfers between devices, along_y(): return lax.ppermute(x, 'fsdp', route)  6.61 us
    all_to_all x3, waiting for transfers between devices, exchange(): return lax.all_to_all(x, 'fsdp', 0, 0, axis_index_groups=groups, tiled=True)  6.47 us
    pallas_call x1, Pallas kernels, apply_whole(): pl.pallas_call(kernel, name='apply_whole', in_specs=[HBM] * (7 + len(root...  4.71 us
    pallas_call x1, Pallas kernels, grams(): pl.pallas_call(kernel, name='grams', in_specs=[HBM] * 7, out_specs=[HBM]...  4.43 us
    pallas_call x1, Pallas kernels, apply_band(): pl.pallas_call(kernel, name='apply_band', in_specs=[HBM] * 6, out_specs=H...  4.36 us
    ppermute x5, starting transfers between devices, along_x(): lax.ppermute(x, 'rep', [(i, (i + distance) % REPLICAS) for i in range(REP...  4.14 us
  transfers between devices with their start and end apart: 15, of which 7 were waited for; matrix products, arithmetic and copies ran while one was open for 0% of the time, Pallas kernels for 25%

profile of v4, /device:TPU:1, one launch (start us, length us, event | category | flops | bytes accessed | tf_op | source)
XLA Modules:
  0.0 79.6 jit_solution(10395339462833196761)
XLA Ops:
  0.6 2.4 %deal.1 = f32[8,64,1024]{2,1,0:T(8,128)} custom-call(f32[64,12288]{1,0:T(8,128)} %grad.5), custom_call_target="tpu_custom_call" | custom-call | flops 1 | bytes 1 | tf_op jit(solution)/shard_map/deal/pallas_call | solution.py:113
  3.0 7.5 %all-to-all-start = ((f32[8,64,1024]{2,1,0:T(8,128)}), f32[8,64,1024]{2,1,0:T(8,128)}, u32[]{:S(2)}, u32[]{:S(2)}) async-start(f32[8,64,1024]{2,1,0:T(8,128)} %deal.1), calls=%async_computation | async-start | bytes 4194304 | tf_op jit(solution)/shard_map/all_to_all | solution.py:434
  10.5 1.8 %deal_core.1 = f32[4,64,512]{2,1,0:T(8,128)} custom-call(f32[64,12288]{1,0:T(8,128)} %grad.5), custom_call_target="tpu_custom_call" | custom-call | flops 1 | bytes 1 | tf_op jit(solution)/shard_map/deal_core/pallas_call | solution.py:134
  12.6 2.5 %pack_roots.1 = (f32[4,128,128]{2,1,0:T(8,128)}, f32[5,128,128]{2,1,0:T(8,128)}, f32[5,128,128]{2,1,0:T(8,128)}, f32[5,128,128]{2,1,0:T(8,128)}, f32[5,128,128]{2,1,0:T(8,128)}) custom-call(f32[3,128,512]{2,1,0:T(8,128)} %refs_4_.1, f32[3,128,512]{2,1,0:T(8,128)} %refs_5_.1), custom_call_target="tpu_custom_call" | custom-call | flops 1 | bytes 1 | tf_op jit(solution)/shard_map/pack_roots/pallas_call | solution.py:190
  15.1 1.2 %collective-permute-start.2 = (f32[4,128,128]{2,1,0:T(8,128)}, f32[4,128,128]{2,1,0:T(8,128)S(1)}, u32[]{:S(2)}, u32[]{:S(2)}) collective-permute-start(f32[4,128,128]{2,1,0:T(8,128)} %get-tuple-element.24), channel_id=1, source_target_pairs={{0,2},{1,3},{2,0},{3,1},{4,6},{5,7},{6,4},{7,5},{8,10},{9,11},{10,... | collective-permute-start | bytes 786440 | tf_op jit(solution)/shard_map/ppermute | solution.py:441
  17.8 6.7 %collective-permute-done.2.refs_5_.refs_1_.refs_8_ = f32[4,128,128]{2,1,0:T(8,128)S(1)} collective-permute-done((f32[4,128,128]{2,1,0:T(8,128)}, f32[4,128,128]{2,1,0:T(8,128)S(1)}, u32[]{:S(2)}, u32[]{:S(2)}) %collective-permute-start.2) | collective-permute-done | bytes 262176 | tf_op jit(solution)/shard_map/ppermute | solution.py:441
  26.6 2.1 %pack.1 = (f32[2,64,512]{2,1,0:T(8,128)}, f32[2,64,512]{2,1,0:T(8,128)}, f32[2,64,512]{2,1,0:T(8,128)}, f32[2,64,512]{2,1,0:T(8,128)}) custom-call(f32[64,12288]{1,0:T(8,128)} %grad.5, f32[4,64,512]{2,1,0:T(8,128)} %collective-permute-done.3.got), custom_call_target="tpu_custom_call" | custom-call | flops 1 | bytes 1 | tf_op jit(solution)/shard_map/pack/pallas_call | solution.py:158
  28.7 1.9 %collective-permute-start.4 = (f32[2,64,512]{2,1,0:T(8,128)}, f32[2,64,512]{2,1,0:T(8,128)S(1)}, u32[]{:S(2)}, u32[]{:S(2)}) collective-permute-start(f32[2,64,512]{2,1,0:T(8,128)} %get-tuple-element.26), channel_id=1, source_target_pairs={{0,8},{4,12},{8,16},{12,20},{16,24},{20,28},{24,0},{28,4},{32,40},... | collective-permute-start | bytes 786440 | tf_op jit(solution)/shard_map/ppermute | solution.py:438
  30.6 2.6 %collective-permute-start.5 = (f32[2,64,512]{2,1,0:T(8,128)}, f32[2,64,512]{2,1,0:T(8,128)}, u32[]{:S(2)}, u32[]{:S(2)}) collective-permute-start(f32[2,64,512]{2,1,0:T(8,128)} %get-tuple-element.27), channel_id=1, source_target_pairs={{0,24},{4,28},{8,0},{12,4},{16,8},{20,12},{24,16},{28,20},{32,56},... | collective-permute-start | bytes 786440 | tf_op jit(solution)/shard_map/ppermute | solution.py:438
  33.2 2.1 %collective-permute-start.6 = (f32[2,64,512]{2,1,0:T(8,128)}, f32[2,64,512]{2,1,0:T(8,128)}, u32[]{:S(2)}, u32[]{:S(2)}) collective-permute-start(f32[2,64,512]{2,1,0:T(8,128)} %get-tuple-element.28), channel_id=1, source_target_pairs={{0,16},{4,20},{8,24},{12,28},{16,0},{20,4},{24,8},{28,12},{32,48},... | collective-permute-start | bytes 786440 | tf_op jit(solution)/shard_map/ppermute | solution.py:438
  35.4 1.6 %all-to-all-done = f32[8,64,1024]{2,1,0:T(8,128)} async-done(((f32[8,64,1024]{2,1,0:T(8,128)}), f32[8,64,1024]{2,1,0:T(8,128)}, u32[]{:S(2)}, u32[]{:S(2)}) %all-to-all-start) | async-done | bytes 2097184 | tf_op jit(solution)/shard_map/all_to_all | solution.py:434
  37.0 4.4 %apply_band.1 = f32[512,256]{1,0:T(8,128)} custom-call(f32[512,1024]{1,0:T(8,128)} %bitcast.refs_0_.blocks, f32[3,128,512]{2,1,0:T(8,128)} %refs_4_.1, f32[3,128,512]{2,1,0:T(8,128)} %refs_5_.1, f32[5,128,128]{2,1,0:T(8,128)} %collective-permute-done.refs_3_, f32[5,128,128]{2,1,0:T(8,128)} %collective-permute-done.1.refs_4_, f32[4,128,128]{2,1,0:T(8,128)} %copy-done.5), custom_call_target="tpu_custom_call" | custom-call | flops 1 | bytes 1 | tf_op jit(solution)/shard_map/apply_band/pallas_call | solution.py:280
  41.4 5.4 %all-to-all-start.1 = ((f32[8,64,256]{2,1,0:T(8,128)}), f32[8,64,256]{2,1,0:T(8,128)}, u32[]{:S(2)}, u32[]{:S(2)}) async-start(f32[8,64,256]{2,1,0:T(8,128)} %bitcast.3), calls=%async_computation.1 | async-start | bytes 1048576 | tf_op jit(solution)/shard_map/all_to_all | solution.py:434
  46.8 1.4 %collective-permute-done.6.refs_3_ = f32[2,64,512]{2,1,0:T(8,128)} collective-permute-done((f32[2,64,512]{2,1,0:T(8,128)}, f32[2,64,512]{2,1,0:T(8,128)}, u32[]{:S(2)}, u32[]{:S(2)}) %collective-permute-start.6) | collective-permute-done | bytes 262176 | tf_op jit(solution)/shard_map/ppermute | solution.py:438
  48.3 4.7 %apply_whole.1 = f32[512,512]{1,0:T(8,128)} custom-call(f32[2,64,512]{2,1,0:T(8,128)} %get-tuple-element.25.refs_0_, f32[2,64,512]{2,1,0:T(8,128)} %copy-done.3, f32[2,64,512]{2,1,0:T(8,128)} %collective-permute-done.5.refs_2_, f32[2,64,512]{2,1,0:T(8,128)} %collective-permute-done.6.refs_3_, f32[3,128,512]{2,1,0:T(8,128)} %refs_4_.1, ...), custom_call_target="tpu_custom_call" | custom-call | flops 137438953472 | bytes 4194304 | tf_op jit(solution)/shard_map/apply_whole/pallas_call | solution.py:328
  53.0 3.4 %all-to-all-done.1.own = f32[8,64,256]{2,1,0:T(8,128)} async-done(((f32[8,64,256]{2,1,0:T(8,128)}), f32[8,64,256]{2,1,0:T(8,128)}, u32[]{:S(2)}, u32[]{:S(2)}) %all-to-all-start.1) | async-done | bytes 524320 | tf_op jit(solution)/shard_map/all_to_all | solution.py:434
  57.3 3.5 %all-to-all-start.2 = ((f32[8,64,512]{2,1,0:T(8,128)}), f32[8,64,512]{2,1,0:T(8,128)S(1)}, u32[]{:S(2)}, u32[]{:S(2)}) async-start(f32[8,64,512]{2,1,0:T(8,128)} %bitcast.4), calls=%async_computation.2 | async-start | bytes 2097152 | tf_op jit(solution)/shard_map/all_to_all | solution.py:434
  61.9 3.4 %collective-permute-done.9.near = f32[8,64,256]{2,1,0:T(8,128)S(1)} collective-permute-done((f32[8,64,256]{2,1,0:T(8,128)}, f32[8,64,256]{2,1,0:T(8,128)S(1)}, u32[]{:S(2)}, u32[]{:S(2)}) %collective-permute-start.9) | collective-permute-done | bytes 524320 | tf_op jit(solution)/shard_map/ppermute | solution.py:445
  65.3 1.5 %collective-permute-start.11 = (f32[8,64,256]{2,1,0:T(8,128)S(1)}, f32[8,64,256]{2,1,0:T(8,128)S(1)}, u32[]{:S(2)}, u32[]{:S(2)}) collective-permute-start(f32[8,64,256]{2,1,0:T(8,128)S(1)} %collective-permute-done.9.near), channel_id=1, source_target_pairs={{0,1},{1,2},{2,3},{3,0},{4,7},{5,4},{6,5},{7,6},{8,9},{9,10},{10,1... | collective-permute-start | bytes 1572872 | tf_op jit(solution)/shard_map/ppermute | solution.py:445
  66.8 1.1 %copy-done = f32[3,128,512]{2,1,0:T(8,128)S(1)} copy-done((f32[3,128,512]{2,1,0:T(8,128)S(1)}, f32[3,128,512]{2,1,0:T(8,128)}, u32[]{:S(2)}) %copy-start) | copy-done | bytes 786456
  67.9 1.1 %copy-done.1 = f32[3,128,512]{2,1,0:T(8,128)S(1)} copy-done((f32[3,128,512]{2,1,0:T(8,128)S(1)}, f32[3,128,512]{2,1,0:T(8,128)}, u32[]{:S(2)}) %copy-start.1) | copy-done | bytes 786456
  70.0 4.4 %grams.1 = (f32[3,128,512]{2,1,0:T(8,128)}, f32[3,128,512]{2,1,0:T(8,128)}) custom-call(f32[512,1024]{1,0:T(8,128)} %bitcast.refs_0_.blocks, f32[2,64,512]{2,1,0:T(8,128)S(1)} %copy-done.2, f32[2,64,512]{2,1,0:T(8,128)S(1)} %copy-done.4, f32[2,64,512]{2,1,0:T(8,128)} %collective-permute-done.5.refs_2_, f32[2,64,512]{2,1,0:T(8,128)} %collective-permute-done.6.refs_3_, ...), custom_call_target="tpu_custom_call" | custom-call | flops 1 | bytes 1 | tf_op jit(solution)/shard_map/grams/pallas_call | solution.py:372
  74.5 1.4 %all-to-all-done.2.filled = f32[8,64,512]{2,1,0:T(8,128)S(1)} async-done(((f32[8,64,512]{2,1,0:T(8,128)}), f32[8,64,512]{2,1,0:T(8,128)S(1)}, u32[]{:S(2)}, u32[]{:S(2)}) %all-to-all-start.2) | async-done | bytes 1048608 | tf_op jit(solution)/shard_map/all_to_all | solution.py:434
  76.5 2.9 %join.1 = f32[64,12288]{1,0:T(8,128)} custom-call(f32[8,64,256]{2,1,0:T(8,128)} %all-to-all-done.1.own, f32[8,64,256]{2,1,0:T(8,128)S(1)} %collective-permute-done.9.near, f32[8,64,256]{2,1,0:T(8,128)S(1)} %collective-permute-done.10.other, f32[8,64,256]{2,1,0:T(8,128)S(1)} %collective-permute-done.11.far, f32[8,64,512]{2,1,0:T(8,128)S(1)} %all-to-all-done.2.filled), custom_call_target="tpu_custom_call" | custom-call | flops 1 | bytes 1 | tf_op jit(solution)/shard_map/join/pallas_call | solution.py:413
  (28 shorter events, 7.4 us)
Async XLA Ops:
  3.0 34.0 %all-to-all-start = ((f32[8,64,1024]{2,1,0:T(8,128)}), f32[8,64,1024]{2,1,0:T(8,128)}, u32[]{:S(2)}, u32[]{:S(2)}) async-start(f32[8,64,1024]{2,1,0:T(8,128)} %deal.1), calls=%async_computation | async-start | bytes 4194304 | tf_op jit(solution)/shard_map/all_to_all | solution.py:434
  12.3 14.3 %collective-permute-start.3 = (f32[4,64,512]{2,1,0:T(8,128)}, f32[4,64,512]{2,1,0:T(8,128)}, u32[]{:S(2)}, u32[]{:S(2)}) collective-permute-start(f32[4,64,512]{2,1,0:T(8,128)} %deal_core.1), channel_id=1, source_target_pairs={{0,4},{4,0},{8,12},{12,8},{16,20},{20,16},{24,28},{28,24},{32,36},... | collective-permute-start | bytes 1572872 | tf_op jit(solution)/shard_map/ppermute | solution.py:448
  15.1 9.4 %collective-permute-start.2 = (f32[4,128,128]{2,1,0:T(8,128)}, f32[4,128,128]{2,1,0:T(8,128)S(1)}, u32[]{:S(2)}, u32[]{:S(2)}) collective-permute-start(f32[4,128,128]{2,1,0:T(8,128)} %get-tuple-element.24), channel_id=1, source_target_pairs={{0,2},{1,3},{2,0},{3,1},{4,6},{5,7},{6,4},{7,5},{8,10},{9,11},{10,... | collective-permute-start | bytes 786440 | tf_op jit(solution)/shard_map/ppermute | solution.py:441
  16.3 14.4 %collective-permute-start = (f32[5,128,128]{2,1,0:T(8,128)}, f32[5,128,128]{2,1,0:T(8,128)}, u32[]{:S(2)}, u32[]{:S(2)}) collective-permute-start(f32[5,128,128]{2,1,0:T(8,128)} %get-tuple-element.22), channel_id=1, source_target_pairs={{0,3},{1,0},{2,1},{3,2},{4,7},{5,4},{6,5},{7,6},{8,11},{9,8},{10,9... | collective-permute-start | bytes 983048 | tf_op jit(solution)/shard_map/ppermute | solution.py:441
  17.2 16.1 %collective-permute-start.1 = (f32[5,128,128]{2,1,0:T(8,128)}, f32[5,128,128]{2,1,0:T(8,128)}, u32[]{:S(2)}, u32[]{:S(2)}) collective-permute-start(f32[5,128,128]{2,1,0:T(8,128)} %get-tuple-element.23), channel_id=1, source_target_pairs={{0,1},{1,2},{2,3},{3,0},{4,5},{5,6},{6,7},{7,4},{8,9},{9,10},{10,1... | collective-permute-start | bytes 983048 | tf_op jit(solution)/shard_map/ppermute | solution.py:441
  24.5 0.7 copy-start.5
  25.2 21.6 %collective-permute-start.7 = (f32[5,128,128]{2,1,0:T(8,128)}, f32[5,128,128]{2,1,0:T(8,128)}, u32[]{:S(2)}, u32[]{:S(2)}) collective-permute-start(f32[5,128,128]{2,1,0:T(8,128)} %follow.2), channel_id=1, source_target_pairs={{0,3},{1,0},{2,1},{3,2},{4,7},{5,4},{6,5},{7,6},{8,11},{9,8},{10,9... | collective-permute-start | bytes 983048 | tf_op jit(solution)/shard_map/ppermute | solution.py:441
  25.9 20.9 %collective-permute-start.8 = (f32[5,128,128]{2,1,0:T(8,128)}, f32[5,128,128]{2,1,0:T(8,128)}, u32[]{:S(2)}, u32[]{:S(2)}) collective-permute-start(f32[5,128,128]{2,1,0:T(8,128)} %follow.3), channel_id=1, source_target_pairs={{0,1},{1,2},{2,3},{3,0},{4,5},{5,6},{6,7},{7,4},{8,9},{9,10},{10,1... | collective-permute-start | bytes 983048 | tf_op jit(solution)/shard_map/ppermute | solution.py:441
  28.7 18.1 %collective-permute-start.4 = (f32[2,64,512]{2,1,0:T(8,128)}, f32[2,64,512]{2,1,0:T(8,128)S(1)}, u32[]{:S(2)}, u32[]{:S(2)}) collective-permute-start(f32[2,64,512]{2,1,0:T(8,128)} %get-tuple-element.26), channel_id=1, source_target_pairs={{0,8},{4,12},{8,16},{12,20},{16,24},{20,28},{24,0},{28,4},{32,40},... | collective-permute-start | bytes 786440 | tf_op jit(solution)/shard_map/ppermute | solution.py:438
  30.6 16.2 %collective-permute-start.5 = (f32[2,64,512]{2,1,0:T(8,128)}, f32[2,64,512]{2,1,0:T(8,128)}, u32[]{:S(2)}, u32[]{:S(2)}) collective-permute-start(f32[2,64,512]{2,1,0:T(8,128)} %get-tuple-element.27), channel_id=1, source_target_pairs={{0,24},{4,28},{8,0},{12,4},{16,8},{20,12},{24,16},{28,20},{32,56},... | collective-permute-start | bytes 786440 | tf_op jit(solution)/shard_map/ppermute | solution.py:438
  33.2 15.0 %collective-permute-start.6 = (f32[2,64,512]{2,1,0:T(8,128)}, f32[2,64,512]{2,1,0:T(8,128)}, u32[]{:S(2)}, u32[]{:S(2)}) collective-permute-start(f32[2,64,512]{2,1,0:T(8,128)} %get-tuple-element.28), channel_id=1, source_target_pairs={{0,16},{4,20},{8,24},{12,28},{16,0},{20,4},{24,8},{28,12},{32,48},... | collective-permute-start | bytes 786440 | tf_op jit(solution)/shard_map/ppermute | solution.py:438
  41.4 15.0 %all-to-all-start.1 = ((f32[8,64,256]{2,1,0:T(8,128)}), f32[8,64,256]{2,1,0:T(8,128)}, u32[]{:S(2)}, u32[]{:S(2)}) async-start(f32[8,64,256]{2,1,0:T(8,128)} %bitcast.3), calls=%async_computation.1 | async-start | bytes 1048576 | tf_op jit(solution)/shard_map/all_to_all | solution.py:434
  46.8 1.4 %copy-start.3 = (f32[2,64,512]{2,1,0:T(8,128)}, f32[2,64,512]{2,1,0:T(8,128)S(1)}, u32[]{:S(2)}) copy-start(f32[2,64,512]{2,1,0:T(8,128)S(1)} %collective-permute-done.4.refs_1_) | copy-start | bytes 786436
  48.3 18.5 %copy-start.2 = (f32[2,64,512]{2,1,0:T(8,128)S(1)}, f32[2,64,512]{2,1,0:T(8,128)}, u32[]{:S(2)}) copy-start(f32[2,64,512]{2,1,0:T(8,128)} %get-tuple-element.25.refs_0_) | copy-start | bytes 786436
  56.4 8.9 %collective-permute-start.9 = (f32[8,64,256]{2,1,0:T(8,128)}, f32[8,64,256]{2,1,0:T(8,128)S(1)}, u32[]{:S(2)}, u32[]{:S(2)}) collective-permute-start(f32[8,64,256]{2,1,0:T(8,128)} %all-to-all-done.1.own), channel_id=1, source_target_pairs={{0,1},{1,2},{2,3},{3,0},{4,7},{5,4},{6,5},{7,6},{8,9},{9,10},{10,1... | collective-permute-start | bytes 1572872 | tf_op jit(solution)/shard_map/ppermute | solution.py:445
  57.3 18.5 %all-to-all-start.2 = ((f32[8,64,512]{2,1,0:T(8,128)}), f32[8,64,512]{2,1,0:T(8,128)S(1)}, u32[]{:S(2)}, u32[]{:S(2)}) async-start(f32[8,64,512]{2,1,0:T(8,128)} %bitcast.4), calls=%async_computation.2 | async-start | bytes 2097152 | tf_op jit(solution)/shard_map/all_to_all | solution.py:434
  60.8 13.6 %collective-permute-start.10 = (f32[8,64,256]{2,1,0:T(8,128)}, f32[8,64,256]{2,1,0:T(8,128)S(1)}, u32[]{:S(2)}, u32[]{:S(2)}) collective-permute-start(f32[8,64,256]{2,1,0:T(8,128)} %all-to-all-done.1.own), channel_id=1, source_target_pairs={{0,3},{1,0},{2,1},{3,2},{4,5},{5,6},{6,7},{7,4},{8,11},{9,8},{10,9... | collective-permute-start | bytes 1572872 | tf_op jit(solution)/shard_map/ppermute | solution.py:445
  65.3 11.1 %collective-permute-start.11 = (f32[8,64,256]{2,1,0:T(8,128)S(1)}, f32[8,64,256]{2,1,0:T(8,128)S(1)}, u32[]{:S(2)}, u32[]{:S(2)}) collective-permute-start(f32[8,64,256]{2,1,0:T(8,128)S(1)} %collective-permute-done.9.near), channel_id=1, source_target_pairs={{0,1},{1,2},{2,3},{3,0},{4,7},{5,4},{6,5},{7,6},{8,9},{9,10},{10,1... | collective-permute-start | bytes 1572872 | tf_op jit(solution)/shard_map/ppermute | solution.py:445
  66.8 1.1 %copy-start = (f32[3,128,512]{2,1,0:T(8,128)S(1)}, f32[3,128,512]{2,1,0:T(8,128)}, u32[]{:S(2)}) copy-start(f32[3,128,512]{2,1,0:T(8,128)} %refs_4_.2) | copy-start | bytes 2359300
  67.9 1.1 %copy-start.1 = (f32[3,128,512]{2,1,0:T(8,128)S(1)}, f32[3,128,512]{2,1,0:T(8,128)}, u32[]{:S(2)}) copy-start(f32[3,128,512]{2,1,0:T(8,128)} %refs_5_.2) | copy-start | bytes 2359300
  69.1 0.9 %copy-start.4 = (f32[2,64,512]{2,1,0:T(8,128)S(1)}, f32[2,64,512]{2,1,0:T(8,128)}, u32[]{:S(2)}) copy-start(f32[2,64,512]{2,1,0:T(8,128)} %copy-done.3) | copy-start | bytes 786436

commit v5 on v4

--- a/solution.py
+++ b/solution.py
@@ -138,7 +138,7 @@
         out_specs=HBM,
         out_shape=array(4, 64, BLOCK),
         scratch_shapes=[pltpu.VMEM((4, 64, BLOCK), F32), dma(8)],
-        compiler_params=PARAMS,
+        compiler_params=SMALL,
         cost_estimate=cost(0, 1 << 20),
     )(grad)
 
@@ -194,7 +194,7 @@
         out_specs=[HBM] * 5,
         out_shape=[array(4, BAND, BAND)] + [array(5, BAND, BAND)] * 4,
         scratch_shapes=[pltpu.VMEM((4, BAND, BLOCK), F32), dma(24)],
-        compiler_params=PARAMS,
+        compiler_params=SMALL,
         cost_estimate=cost(0, 2 << 20),
     )(*roots)
 

time: 80.9 us -> 81.1 us (level)
  Pallas kernels: 25.3 us -> 23 us
  local copies, waits for them, and re-layouts: 3.92 us -> 5.73 us
  waiting for transfers between devices: 18.7 us -> 19.8 us
    unnamed x12 -> x22, local copies, waits for them, and re-layouts: 3.92 us -> 5.73 us
    pallas_call x1, Pallas kernels: 2.51 us -> 1.12 us  [pack_roots(): pl.pallas_call(kernel, name='pack_roots', in_specs=[HBM] * len(roots), ou...]
    all_to_all x3, waiting for transfers between devices: 6.47 us -> 7.36 us  [exchange(): return lax.all_to_all(x, 'fsdp', 0, 0, axis_index_groups=groups, tiled=True)]
    pallas_call x1, Pallas kernels: 1.82 us -> 0.96 us  [deal_core(): pl.pallas_call(kernel, name='deal_core', in_specs=[HBM], out_specs=HBM, o...]
  transfers between devices with their start and end apart: 15 -> 15, of which waited for: 7 -> 8; matrix products, arithmetic and copies ran while one was open for 0% -> 0% of each run, Pallas kernels for 25% -> 22%
where the time goes in v5:
time: 81.1 us; the launch traced here: 79.8 us
  starting transfers between devices  30.3 us (37%)
  Pallas kernels  23 us (28%)
  waiting for transfers between devices  19.8 us (24%)
  local copies, waits for them, and re-layouts  5.73 us (7%)
  between operations  0.93 us (1%)
    all_to_all x3, starting transfers between devices, exchange(): return lax.all_to_all(x, 'fsdp', 0, 0, axis_index_groups=groups, tiled=True)  16.6 us
    all_to_all x3, waiting for transfers between devices, exchange(): return lax.all_to_all(x, 'fsdp', 0, 0, axis_index_groups=groups, tiled=True)  7.36 us
    ppermute x5, waiting for transfers between devices, along_x(): lax.ppermute(x, 'rep', [(i, (i + distance) % REPLICAS) for i in range(REP...  6.93 us
    ppermute x3, starting transfers between devices, along_y(): return lax.ppermute(x, 'fsdp', route)  5.83 us
    unnamed x22, local copies, waits for them, and re-layouts  5.73 us
    pallas_call x1, Pallas kernels, apply_whole(): pl.pallas_call(kernel, name='apply_whole', in_specs=[HBM] * (7 + len(root...  4.71 us
    pallas_call x1, Pallas kernels, grams(): pl.pallas_call(kernel, name='grams', in_specs=[HBM] * 7, out_specs=[HBM]...  4.43 us
    pallas_call x1, Pallas kernels, apply_band(): pl.pallas_call(kernel, name='apply_band', in_specs=[HBM] * 6, out_specs=H...  4.39 us
  transfers between devices with their start and end apart: 15, of which 8 were waited for; matrix products, arithmetic and copies ran while one was open for 0% of the time, Pallas kernels for 22%

profile of v5, /device:TPU:1, one launch (start us, length us, event | category | flops | bytes accessed | tf_op | source)
XLA Modules:
  0.0 79.8 jit_solution(8289227600390667728)
XLA Ops:
  0.6 2.4 %deal.1 = f32[8,64,1024]{2,1,0:T(8,128)} custom-call(f32[64,12288]{1,0:T(8,128)} %grad.5), custom_call_target="tpu_custom_call" | custom-call | flops 1 | bytes 1 | tf_op jit(solution)/shard_map/deal/pallas_call | solution.py:113
  3.0 7.7 %all-to-all-start = ((f32[8,64,1024]{2,1,0:T(8,128)}), f32[8,64,1024]{2,1,0:T(8,128)}, u32[]{:S(2)}, u32[]{:S(2)}) async-start(f32[8,64,1024]{2,1,0:T(8,128)} %deal.1), calls=%async_computation | async-start | bytes 4194304 | tf_op jit(solution)/shard_map/all_to_all | solution.py:434
  12.3 1.1 %pack_roots.1 = (f32[4,128,128]{2,1,0:T(8,128)S(1)}, f32[5,128,128]{2,1,0:T(8,128)}, f32[5,128,128]{2,1,0:T(8,128)}, f32[5,128,128]{2,1,0:T(8,128)S(1)}, f32[5,128,128]{2,1,0:T(8,128)S(1)}) custom-call(f32[3,128,512]{2,1,0:T(8,128)S(1)} %copy-done.1, f32[3,128,512]{2,1,0:T(8,128)S(1)} %copy-done.2), custom_call_target="tpu_custom_call" | custom-call | flops 1 | bytes 1 | tf_op jit(solution)/shard_map/pack_roots/pallas_call | solution.py:190
  14.9 1.2 %collective-permute-start.2 = (f32[4,128,128]{2,1,0:T(8,128)S(1)}, f32[4,128,128]{2,1,0:T(8,128)S(1)}, u32[]{:S(2)}, u32[]{:S(2)}) collective-permute-start(f32[4,128,128]{2,1,0:T(8,128)S(1)} %get-tuple-element.24), channel_id=1, source_target_pairs={{0,2},{1,3},{2,0},{3,1},{4,6},{5,7},{6,4},{7,5},{8,10},{9,11},{10,... | collective-permute-start | bytes 786440 | tf_op jit(solution)/shard_map/ppermute | solution.py:441
  17.6 6.6 %collective-permute-done.2.refs_5_.refs_1_.refs_8_ = f32[4,128,128]{2,1,0:T(8,128)S(1)} collective-permute-done((f32[4,128,128]{2,1,0:T(8,128)S(1)}, f32[4,128,128]{2,1,0:T(8,128)S(1)}, u32[]{:S(2)}, u32[]{:S(2)}) %collective-permute-start.2) | collective-permute-done | bytes 262176 | tf_op jit(solution)/shard_map/ppermute | solution.py:441
  25.0 1.1 %collective-permute-start.7 = (f32[5,128,128]{2,1,0:T(8,128)}, f32[5,128,128]{2,1,0:T(8,128)}, u32[]{:S(2)}, u32[]{:S(2)}) collective-permute-start(f32[5,128,128]{2,1,0:T(8,128)} %follow.2), channel_id=1, source_target_pairs={{0,3},{1,0},{2,1},{3,2},{4,7},{5,4},{6,5},{7,6},{8,11},{9,8},{10,9... | collective-permute-start | bytes 983048 | tf_op jit(solution)/shard_map/ppermute | solution.py:441
  26.4 2.1 %pack.1 = (f32[2,64,512]{2,1,0:T(8,128)}, f32[2,64,512]{2,1,0:T(8,128)}, f32[2,64,512]{2,1,0:T(8,128)}, f32[2,64,512]{2,1,0:T(8,128)}) custom-call(f32[64,12288]{1,0:T(8,128)} %grad.5, f32[4,64,512]{2,1,0:T(8,128)} %collective-permute-done.3.got), custom_call_target="tpu_custom_call" | custom-call | flops 1 | bytes 1 | tf_op jit(solution)/shard_map/pack/pallas_call | solution.py:158
  28.5 1.2 %collective-permute-start.4 = (f32[2,64,512]{2,1,0:T(8,128)}, f32[2,64,512]{2,1,0:T(8,128)S(1)}, u32[]{:S(2)}, u32[]{:S(2)}) collective-permute-start(f32[2,64,512]{2,1,0:T(8,128)} %get-tuple-element.26), channel_id=1, source_target_pairs={{0,8},{4,12},{8,16},{12,20},{16,24},{20,28},{24,0},{28,4},{32,40},... | collective-permute-start | bytes 786440 | tf_op jit(solution)/shard_map/ppermute | solution.py:438
  30.1 2.2 %collective-permute-start.5 = (f32[2,64,512]{2,1,0:T(8,128)}, f32[2,64,512]{2,1,0:T(8,128)}, u32[]{:S(2)}, u32[]{:S(2)}) collective-permute-start(f32[2,64,512]{2,1,0:T(8,128)} %get-tuple-element.27), channel_id=1, source_target_pairs={{0,24},{4,28},{8,0},{12,4},{16,8},{20,12},{24,16},{28,20},{32,56},... | collective-permute-start | bytes 786440 | tf_op jit(solution)/shard_map/ppermute | solution.py:438
  32.3 2.4 %collective-permute-start.6 = (f32[2,64,512]{2,1,0:T(8,128)}, f32[2,64,512]{2,1,0:T(8,128)}, u32[]{:S(2)}, u32[]{:S(2)}) collective-permute-start(f32[2,64,512]{2,1,0:T(8,128)} %get-tuple-element.28), channel_id=1, source_target_pairs={{0,16},{4,20},{8,24},{12,28},{16,0},{20,4},{24,8},{28,12},{32,48},... | collective-permute-start | bytes 786440 | tf_op jit(solution)/shard_map/ppermute | solution.py:438
  34.7 2.6 %all-to-all-done = f32[8,64,1024]{2,1,0:T(8,128)} async-done(((f32[8,64,1024]{2,1,0:T(8,128)}), f32[8,64,1024]{2,1,0:T(8,128)}, u32[]{:S(2)}, u32[]{:S(2)}) %all-to-all-start) | async-done | bytes 2097184 | tf_op jit(solution)/shard_map/all_to_all | solution.py:434
  37.3 4.4 %apply_band.1 = f32[512,256]{1,0:T(8,128)} custom-call(f32[512,1024]{1,0:T(8,128)} %bitcast.refs_0_.blocks, f32[3,128,512]{2,1,0:T(8,128)} %refs_4_.1, f32[3,128,512]{2,1,0:T(8,128)} %refs_5_.1, f32[5,128,128]{2,1,0:T(8,128)} %collective-permute-done.refs_3_, f32[5,128,128]{2,1,0:T(8,128)} %collective-permute-done.1.refs_4_, f32[4,128,128]{2,1,0:T(8,128)} %copy-done.10), custom_call_target="tpu_custom_call" | custom-call | flops 1 | bytes 1 | tf_op jit(solution)/shard_map/apply_band/pallas_call | solution.py:280
  41.7 5.3 %all-to-all-start.1 = ((f32[8,64,256]{2,1,0:T(8,128)}), f32[8,64,256]{2,1,0:T(8,128)}, u32[]{:S(2)}, u32[]{:S(2)}) async-start(f32[8,64,256]{2,1,0:T(8,128)} %bitcast.3), calls=%async_computation.1 | async-start | bytes 1048576 | tf_op jit(solution)/shard_map/all_to_all | solution.py:434
  47.1 1.5 %collective-permute-done.6.refs_3_ = f32[2,64,512]{2,1,0:T(8,128)} collective-permute-done((f32[2,64,512]{2,1,0:T(8,128)}, f32[2,64,512]{2,1,0:T(8,128)}, u32[]{:S(2)}, u32[]{:S(2)}) %collective-permute-start.6) | collective-permute-done | bytes 262176 | tf_op jit(solution)/shard_map/ppermute | solution.py:438
  48.5 4.7 %apply_whole.1 = f32[512,512]{1,0:T(8,128)} custom-call(f32[2,64,512]{2,1,0:T(8,128)} %get-tuple-element.25.refs_0_, f32[2,64,512]{2,1,0:T(8,128)} %copy-done.8, f32[2,64,512]{2,1,0:T(8,128)} %collective-permute-done.5.refs_2_, f32[2,64,512]{2,1,0:T(8,128)} %collective-permute-done.6.refs_3_, f32[3,128,512]{2,1,0:T(8,128)} %refs_4_.1, ...), custom_call_target="tpu_custom_call" | custom-call | flops 137438953472 | bytes 4194304 | tf_op jit(solution)/shard_map/apply_whole/pallas_call | solution.py:328
  53.2 3.4 %all-to-all-done.1.own = f32[8,64,256]{2,1,0:T(8,128)} async-done(((f32[8,64,256]{2,1,0:T(8,128)}), f32[8,64,256]{2,1,0:T(8,128)}, u32[]{:S(2)}, u32[]{:S(2)}) %all-to-all-start.1) | async-done | bytes 524320 | tf_op jit(solution)/shard_map/all_to_all | solution.py:434
  57.6 3.5 %all-to-all-start.2 = ((f32[8,64,512]{2,1,0:T(8,128)}), f32[8,64,512]{2,1,0:T(8,128)S(1)}, u32[]{:S(2)}, u32[]{:S(2)}) async-start(f32[8,64,512]{2,1,0:T(8,128)} %bitcast.4), calls=%async_computation.2 | async-start | bytes 2097152 | tf_op jit(solution)/shard_map/all_to_all | solution.py:434
  62.2 3.4 %collective-permute-done.9.near = f32[8,64,256]{2,1,0:T(8,128)S(1)} collective-permute-done((f32[8,64,256]{2,1,0:T(8,128)}, f32[8,64,256]{2,1,0:T(8,128)S(1)}, u32[]{:S(2)}, u32[]{:S(2)}) %collective-permute-start.9) | collective-permute-done | bytes 524320 | tf_op jit(solution)/shard_map/ppermute | solution.py:445
  65.6 1.5 %collective-permute-start.11 = (f32[8,64,256]{2,1,0:T(8,128)S(1)}, f32[8,64,256]{2,1,0:T(8,128)S(1)}, u32[]{:S(2)}, u32[]{:S(2)}) collective-permute-start(f32[8,64,256]{2,1,0:T(8,128)S(1)} %collective-permute-done.9.near), channel_id=1, source_target_pairs={{0,1},{1,2},{2,3},{3,0},{4,7},{5,4},{6,5},{7,6},{8,9},{9,10},{10,1... | collective-permute-start | bytes 1572872 | tf_op jit(solution)/shard_map/ppermute | solution.py:445
  67.0 1.1 %copy-done.3 = f32[3,128,512]{2,1,0:T(8,128)S(1)} copy-done((f32[3,128,512]{2,1,0:T(8,128)S(1)}, f32[3,128,512]{2,1,0:T(8,128)}, u32[]{:S(2)}) %copy-start.3) | copy-done | bytes 786456
  68.2 1.1 %copy-done.4 = f32[3,128,512]{2,1,0:T(8,128)S(1)} copy-done((f32[3,128,512]{2,1,0:T(8,128)S(1)}, f32[3,128,512]{2,1,0:T(8,128)}, u32[]{:S(2)}) %copy-start.4) | copy-done | bytes 786456
  70.3 4.4 %grams.1 = (f32[3,128,512]{2,1,0:T(8,128)}, f32[3,128,512]{2,1,0:T(8,128)}) custom-call(f32[512,1024]{1,0:T(8,128)} %bitcast.refs_0_.blocks, f32[2,64,512]{2,1,0:T(8,128)S(1)} %copy-done.7, f32[2,64,512]{2,1,0:T(8,128)S(1)} %copy-done.9, f32[2,64,512]{2,1,0:T(8,128)} %collective-permute-done.5.refs_2_, f32[2,64,512]{2,1,0:T(8,128)} %collective-permute-done.6.refs_3_, ...), custom_call_target="tpu_custom_call" | custom-call | flops 1 | bytes 1 | tf_op jit(solution)/shard_map/grams/pallas_call | solution.py:372
  74.7 1.4 %all-to-all-done.2.filled = f32[8,64,512]{2,1,0:T(8,128)S(1)} async-done(((f32[8,64,512]{2,1,0:T(8,128)}), f32[8,64,512]{2,1,0:T(8,128)S(1)}, u32[]{:S(2)}, u32[]{:S(2)}) %all-to-all-start.2) | async-done | bytes 1048608 | tf_op jit(solution)/shard_map/all_to_all | solution.py:434
  76.7 2.9 %join.1 = f32[64,12288]{1,0:T(8,128)} custom-call(f32[8,64,256]{2,1,0:T(8,128)} %all-to-all-done.1.own, f32[8,64,256]{2,1,0:T(8,128)S(1)} %collective-permute-done.9.near, f32[8,64,256]{2,1,0:T(8,128)S(1)} %collective-permute-done.10.other, f32[8,64,256]{2,1,0:T(8,128)S(1)} %collective-permute-done.11.far, f32[8,64,512]{2,1,0:T(8,128)S(1)} %all-to-all-done.2.filled), custom_call_target="tpu_custom_call" | custom-call | flops 1 | bytes 1 | tf_op jit(solution)/shard_map/join/pallas_call | solution.py:413
  (38 shorter events, 9.4 us)
Async XLA Ops:
  3.0 7.8 %copy-start = (f32[64,12288]{1,0:T(8,128)S(1)}, f32[64,12288]{1,0:T(8,128)}, u32[]{:S(2)}) copy-start(f32[64,12288]{1,0:T(8,128)} %grad.5) | copy-start | bytes 9437188
  3.0 34.2 %all-to-all-start = ((f32[8,64,1024]{2,1,0:T(8,128)}), f32[8,64,1024]{2,1,0:T(8,128)}, u32[]{:S(2)}, u32[]{:S(2)}) async-start(f32[8,64,1024]{2,1,0:T(8,128)} %deal.1), calls=%async_computation | async-start | bytes 4194304 | tf_op jit(solution)/shard_map/all_to_all | solution.py:434
  10.8 1.3 %copy-start.1 = (f32[3,128,512]{2,1,0:T(8,128)S(1)}, f32[3,128,512]{2,1,0:T(8,128)}, u32[]{:S(2)}) copy-start(f32[3,128,512]{2,1,0:T(8,128)} %refs_4_.1) | copy-start | bytes 2359300
  10.8 1.6 %copy-start.2 = (f32[3,128,512]{2,1,0:T(8,128)S(1)}, f32[3,128,512]{2,1,0:T(8,128)}, u32[]{:S(2)}) copy-start(f32[3,128,512]{2,1,0:T(8,128)} %refs_5_.1) | copy-start | bytes 2359300
  11.8 14.7 %collective-permute-start.3 = (f32[4,64,512]{2,1,0:T(8,128)}, f32[4,64,512]{2,1,0:T(8,128)}, u32[]{:S(2)}, u32[]{:S(2)}) collective-permute-start(f32[4,64,512]{2,1,0:T(8,128)} %deal_core.1), channel_id=1, source_target_pairs={{0,4},{4,0},{8,12},{12,8},{16,20},{20,16},{24,28},{28,24},{32,36},... | collective-permute-start | bytes 1572872 | tf_op jit(solution)/shard_map/ppermute | solution.py:448
  14.9 9.3 %collective-permute-start.2 = (f32[4,128,128]{2,1,0:T(8,128)S(1)}, f32[4,128,128]{2,1,0:T(8,128)S(1)}, u32[]{:S(2)}, u32[]{:S(2)}) collective-permute-start(f32[4,128,128]{2,1,0:T(8,128)S(1)} %get-tuple-element.24), channel_id=1, source_target_pairs={{0,2},{1,3},{2,0},{3,1},{4,6},{5,7},{6,4},{7,5},{8,10},{9,11},{10,... | collective-permute-start | bytes 786440 | tf_op jit(solution)/shard_map/ppermute | solution.py:441
  16.2 13.9 %collective-permute-start = (f32[5,128,128]{2,1,0:T(8,128)}, f32[5,128,128]{2,1,0:T(8,128)}, u32[]{:S(2)}, u32[]{:S(2)}) collective-permute-start(f32[5,128,128]{2,1,0:T(8,128)} %get-tuple-element.22), channel_id=1, source_target_pairs={{0,3},{1,0},{2,1},{3,2},{4,7},{5,4},{6,5},{7,6},{8,11},{9,8},{10,9... | collective-permute-start | bytes 983048 | tf_op jit(solution)/shard_map/ppermute | solution.py:441
  17.0 15.3 %collective-permute-start.1 = (f32[5,128,128]{2,1,0:T(8,128)}, f32[5,128,128]{2,1,0:T(8,128)}, u32[]{:S(2)}, u32[]{:S(2)}) collective-permute-start(f32[5,128,128]{2,1,0:T(8,128)} %get-tuple-element.23), channel_id=1, source_target_pairs={{0,1},{1,2},{2,3},{3,0},{4,5},{5,6},{6,7},{7,4},{8,9},{9,10},{10,1... | collective-permute-start | bytes 983048 | tf_op jit(solution)/shard_map/ppermute | solution.py:441
  24.2 0.7 copy-start.10
  25.0 22.1 %collective-permute-start.7 = (f32[5,128,128]{2,1,0:T(8,128)}, f32[5,128,128]{2,1,0:T(8,128)}, u32[]{:S(2)}, u32[]{:S(2)}) collective-permute-start(f32[5,128,128]{2,1,0:T(8,128)} %follow.2), channel_id=1, source_target_pairs={{0,3},{1,0},{2,1},{3,2},{4,7},{5,4},{6,5},{7,6},{8,11},{9,8},{10,9... | collective-permute-start | bytes 983048 | tf_op jit(solution)/shard_map/ppermute | solution.py:441
  26.1 20.9 %collective-permute-start.8 = (f32[5,128,128]{2,1,0:T(8,128)}, f32[5,128,128]{2,1,0:T(8,128)}, u32[]{:S(2)}, u32[]{:S(2)}) collective-permute-start(f32[5,128,128]{2,1,0:T(8,128)} %follow.3), channel_id=1, source_target_pairs={{0,1},{1,2},{2,3},{3,0},{4,5},{5,6},{6,7},{7,4},{8,9},{9,10},{10,1... | collective-permute-start | bytes 983048 | tf_op jit(solution)/shard_map/ppermute | solution.py:441
  28.5 18.5 %collective-permute-start.4 = (f32[2,64,512]{2,1,0:T(8,128)}, f32[2,64,512]{2,1,0:T(8,128)S(1)}, u32[]{:S(2)}, u32[]{:S(2)}) collective-permute-start(f32[2,64,512]{2,1,0:T(8,128)} %get-tuple-element.26), channel_id=1, source_target_pairs={{0,8},{4,12},{8,16},{12,20},{16,24},{20,28},{24,0},{28,4},{32,40},... | collective-permute-start | bytes 786440 | tf_op jit(solution)/shard_map/ppermute | solution.py:438
  30.1 17.0 %collective-permute-start.5 = (f32[2,64,512]{2,1,0:T(8,128)}, f32[2,64,512]{2,1,0:T(8,128)}, u32[]{:S(2)}, u32[]{:S(2)}) collective-permute-start(f32[2,64,512]{2,1,0:T(8,128)} %get-tuple-element.27), channel_id=1, source_target_pairs={{0,24},{4,28},{8,0},{12,4},{16,8},{20,12},{24,16},{28,20},{32,56},... | collective-permute-start | bytes 786440 | tf_op jit(solution)/shard_map/ppermute | solution.py:438
  32.3 16.2 %collective-permute-start.6 = (f32[2,64,512]{2,1,0:T(8,128)}, f32[2,64,512]{2,1,0:T(8,128)}, u32[]{:S(2)}, u32[]{:S(2)}) collective-permute-start(f32[2,64,512]{2,1,0:T(8,128)} %get-tuple-element.28), channel_id=1, source_target_pairs={{0,16},{4,20},{8,24},{12,28},{16,0},{20,4},{24,8},{28,12},{32,48},... | collective-permute-start | bytes 786440 | tf_op jit(solution)/shard_map/ppermute | solution.py:438
  41.7 15.0 %all-to-all-start.1 = ((f32[8,64,256]{2,1,0:T(8,128)}), f32[8,64,256]{2,1,0:T(8,128)}, u32[]{:S(2)}, u32[]{:S(2)}) async-start(f32[8,64,256]{2,1,0:T(8,128)} %bitcast.3), calls=%async_computation.1 | async-start | bytes 1048576 | tf_op jit(solution)/shard_map/all_to_all | solution.py:434
  47.0 1.5 %copy-start.8 = (f32[2,64,512]{2,1,0:T(8,128)}, f32[2,64,512]{2,1,0:T(8,128)S(1)}, u32[]{:S(2)}) copy-start(f32[2,64,512]{2,1,0:T(8,128)S(1)} %collective-permute-done.4.refs_1_) | copy-start | bytes 786436
  48.5 18.5 %copy-start.7 = (f32[2,64,512]{2,1,0:T(8,128)S(1)}, f32[2,64,512]{2,1,0:T(8,128)}, u32[]{:S(2)}) copy-start(f32[2,64,512]{2,1,0:T(8,128)} %get-tuple-element.25.refs_0_) | copy-start | bytes 786436
  56.6 8.9 %collective-permute-start.9 = (f32[8,64,256]{2,1,0:T(8,128)}, f32[8,64,256]{2,1,0:T(8,128)S(1)}, u32[]{:S(2)}, u32[]{:S(2)}) collective-permute-start(f32[8,64,256]{2,1,0:T(8,128)} %all-to-all-done.1.own), channel_id=1, source_target_pairs={{0,1},{1,2},{2,3},{3,0},{4,7},{5,4},{6,5},{7,6},{8,9},{9,10},{10,1... | collective-permute-start | bytes 1572872 | tf_op jit(solution)/shard_map/ppermute | solution.py:445
  57.6 18.5 %all-to-all-start.2 = ((f32[8,64,512]{2,1,0:T(8,128)}), f32[8,64,512]{2,1,0:T(8,128)S(1)}, u32[]{:S(2)}, u32[]{:S(2)}) async-start(f32[8,64,512]{2,1,0:T(8,128)} %bitcast.4), calls=%async_computation.2 | async-start | bytes 2097152 | tf_op jit(solution)/shard_map/all_to_all | solution.py:434
  61.1 13.6 %collective-permute-start.10 = (f32[8,64,256]{2,1,0:T(8,128)}, f32[8,64,256]{2,1,0:T(8,128)S(1)}, u32[]{:S(2)}, u32[]{:S(2)}) collective-permute-start(f32[8,64,256]{2,1,0:T(8,128)} %all-to-all-done.1.own), channel_id=1, source_target_pairs={{0,3},{1,0},{2,1},{3,2},{4,5},{5,6},{6,7},{7,4},{8,11},{9,8},{10,9... | collective-permute-start | bytes 1572872 | tf_op jit(solution)/shard_map/ppermute | solution.py:445
  65.6 11.1 %collective-permute-start.11 = (f32[8,64,256]{2,1,0:T(8,128)S(1)}, f32[8,64,256]{2,1,0:T(8,128)S(1)}, u32[]{:S(2)}, u32[]{:S(2)}) collective-permute-start(f32[8,64,256]{2,1,0:T(8,128)S(1)} %collective-permute-done.9.near), channel_id=1, source_target_pairs={{0,1},{1,2},{2,3},{3,0},{4,7},{5,4},{6,5},{7,6},{8,9},{9,10},{10,1... | collective-permute-start | bytes 1572872 | tf_op jit(solution)/shard_map/ppermute | solution.py:445
  67.0 1.1 %copy-start.3 = (f32[3,128,512]{2,1,0:T(8,128)S(1)}, f32[3,128,512]{2,1,0:T(8,128)}, u32[]{:S(2)}) copy-start(f32[3,128,512]{2,1,0:T(8,128)} %refs_4_.2) | copy-start | bytes 2359300
  68.2 1.1 %copy-start.4 = (f32[3,128,512]{2,1,0:T(8,128)S(1)}, f32[3,128,512]{2,1,0:T(8,128)}, u32[]{:S(2)}) copy-start(f32[3,128,512]{2,1,0:T(8,128)} %refs_5_.2) | copy-start | bytes 2359300
  69.3 0.9 %copy-start.9 = (f32[2,64,512]{2,1,0:T(8,128)S(1)}, f32[2,64,512]{2,1,0:T(8,128)}, u32[]{:S(2)}) copy-start(f32[2,64,512]{2,1,0:T(8,128)} %copy-done.8) | copy-start | bytes 786436
  (2 other events, 1.4 us)
